TPU v7x, 256 devices: a whole 4x4x8 slice. The times are simulated.
256 devices in a mesh: mem: 16 (over z, x_lo), tx: 8 (over y, core), ty: 2 (over x_hi).
Axes of the slice: x: 4 (x_hi: 2, x_lo: 2; x = x_hi * 2 + x_lo), y: 4, z: 8, core: 2. Of those that a mesh axis runs over, the one named last changes fastest.
Arguments:
- alpha: float32 [128, 4, 128, 64], P('mem', None, 'tx', 'ty'), may hold values from -6 to 6
- filter_rate: float32 [128, 64], P('tx', 'ty'), may hold values from 0.1 to 0.24
- block_list: int32 [8, 2, 32], P('tx', 'ty'), may hold values from 0 to 127, as said below
- interp_weights: float32 [8, 2, 32, 64, 256], P('tx', 'ty'), may hold values from -0.75 to 0.75
- perturbations: bfloat16 [128, 4, 4, 512, 256], P('mem', None, None, ('tx', 'ty')), may hold values from -1.5 to 1.5
- obs_cells: int32 [8, 2, 512], P('tx', 'ty'), may hold values from 0 to 8191
- obs_count: int32 [8, 2], P('tx', 'ty'), may hold values from 1 to 512, as said below
- departures: float32 [8, 2, 16, 512], P('tx', 'ty', 'mem'), may hold values from -6 to 6
- obs_weight: float32 [8, 2, 16, 512], P('tx', 'ty', 'mem'), may hold values from 0.25 to 2.5
Outputs:
- increment: float32 [16, 512, 256], P('mem', ('tx', 'ty'))
- weighted_departure: float32 [8, 2, 16, 512], P('tx', 'ty', 'mem')
- gradient: float32 [128, 4, 128, 64], P('mem', None, 'tx', 'ty')
Inputs may be any that keep to these rules, and one draw needn't show every extreme that they name: `block_list`: Among the fine blocks of one tile, at most 2 distinct coarse blocks of any one tile are named; every tile names exactly 2 distinct blocks of its own. `obs_count`: some tile has all 512 slots in use in every draw.
All inputs are finite; a program needn't handle non-finite values.
Results may differ from a plain program's by a relative error of at most 0.0003.
Values sent between devices are 32-bit elements; how exact they have to be, the bound alone decides.
A program may use at most 64 MiB of HBM per device.

v0:
```python
import jax
import jax.numpy as jnp
from jax import lax
from jax.sharding import PartitionSpec as P

VARS = 4
CB = 8
SWEEPS = 4
CAP = 2


exact_mode = lax.Precision.HIGHEST


def extended(value, sides, width):
    for axis, dim in sides:
        devices, length = (lax.axis_size(axis), value.shape[dim])
        up = [(i, (i + 1) % devices) for i in range(devices - 1)]
        down = [(j, i) for i, j in up]
        last = lax.slice_in_dim(value, length - width, length, axis=dim)
        leading = lax.slice_in_dim(value, 0, width, axis=dim)
        before = lax.ppermute(last, axis, up)
        after = lax.ppermute(leading, axis, down)
        value = jnp.concatenate([before, value, after], axis=dim)
    return value


def sent_to_all(value, axis):
    devices = lax.axis_size(axis)
    return lax.all_to_all(
        jnp.broadcast_to(value[None], (devices, *value.shape)), axis, 0, 0, tiled=True
    )


def joined_along(blocks, dim):
    blocks = jnp.moveaxis(blocks, 0, dim)
    shape = blocks.shape
    return blocks.reshape(*shape[:dim], shape[dim] * shape[dim + 1], *shape[dim + 2 :])


def collect(value, axis, dim):
    blocks = sent_to_all(value, axis)
    return joined_along(blocks, dim)


def in_blocks(value, dim, devices):
    shape = value.shape
    blocks = value.reshape(*shape[:dim], devices, shape[dim] // devices, *shape[dim + 1 :])
    return jnp.moveaxis(blocks, dim, 0)


def sent_and_summed(value, axis, dim):
    devices = lax.axis_size(axis)
    blocks = lax.all_to_all(in_blocks(value, dim, devices), axis, 0, 0, tiled=True)
    return jnp.sum(blocks, axis=0)


def beside_all(values):
    return values[:, 2:, 1:-1] + values[:, :-2, 1:-1] + values[:, 1:-1, 2:] + values[:, 1:-1, :-2]


def deep_sweeps(values, rate_field, backward):
    stacked = jnp.concatenate([values, rate_field[None]], axis=0)
    padded = extended(stacked, (("tx", 1), ("ty", 2)), SWEEPS)
    field = padded[:-1]
    rates = padded[-1:]
    for sweep_no in range(SWEEPS):
        inner_rate = rates[:, 1:-1, 1:-1]
        center = field[:, 1:-1, 1:-1]
        if backward:
            scaled = rates * field
            field = center + beside_all(scaled) - 4.0 * (inner_rate * center)
        else:
            field = center + inner_rate * (beside_all(field) - 4.0 * center)
        rates = inner_rate
    return field


def to_blocks(values):
    row_count, width_x, width_y = values.shape
    arranged = values.reshape(row_count, width_x // CB, CB, width_y // CB, CB).transpose(
        1, 3, 0, 2, 4
    )
    return arranged.reshape(-1, row_count, CB * CB)


def from_blocks(blocks, width_x, width_y):
    row_count = blocks.shape[1]
    arranged = blocks.reshape(width_x // CB, width_y // CB, row_count, CB, CB).transpose(
        2, 0, 3, 1, 4
    )
    return arranged.reshape(row_count, width_x, width_y)


def on_device(
    alpha,
    filter_rate,
    block_list,
    interp_weights,
    perturbations,
    obs_cells,
    obs_count,
    departures,
    obs_weight,
):
    members, levels, width_x, width_y = alpha.shape
    row_count = members * levels
    coarse = alpha.reshape(row_count, width_x, width_y)
    coarse = deep_sweeps(coarse, filter_rate, False)
    blocks = to_blocks(coarse)
    own_count = blocks.shape[0]
    block_size = CB * CB
    tile_count = lax.axis_size("tx") * lax.axis_size("ty")
    tile_index = lax.axis_index("tx") * lax.axis_size("ty") + lax.axis_index("ty")
    wanted = block_list.reshape(-1)
    fine_count = wanted.shape[0]
    weights = interp_weights.reshape(fine_count, block_size, -1)
    block_cells = weights.shape[2]
    all_lists = collect(wanted[None], ("tx", "ty"), 0)
    own_ids = tile_index * own_count + jnp.arange(own_count, dtype=jnp.int32)
    requested = jnp.any(all_lists[:, :, None] == own_ids[None, None, :], axis=1)
    order_rank = jnp.cumsum(requested.astype(jnp.int32), axis=1) - 1
    cap_ids = jnp.arange(CAP, dtype=jnp.int32)
    chooser = (requested[:, None, :] & (order_rank[:, None, :] == cap_ids[None, :, None])).astype(
        jnp.float32
    )
    outgoing = jnp.einsum(
        "dsk,kq->dsq", chooser, blocks.reshape(own_count, -1), precision=exact_mode
    )
    incoming = lax.all_to_all(outgoing, ("tx", "ty"), split_axis=0, concat_axis=0, tiled=True)
    every_block = jnp.arange(tile_count * own_count, dtype=jnp.int32)
    my_asked = jnp.any(wanted[:, None] == every_block[None, :], axis=0).reshape(
        tile_count, own_count
    )
    my_rank = jnp.cumsum(my_asked.astype(jnp.int32), axis=1) - 1
    slot_of = my_rank.reshape(-1)[wanted]
    position = wanted // own_count * CAP + slot_of
    selector = (position[:, None] == jnp.arange(tile_count * CAP, dtype=jnp.int32)[None, :]).astype(
        jnp.float32
    )
    picked = jnp.dot(
        selector,
        incoming.reshape(tile_count * CAP, -1),
        precision=exact_mode,
        preferred_element_type=jnp.float32,
    )
    fine_alpha = jnp.einsum(
        "frk,fkc->rfc",
        picked.reshape(fine_count, row_count, block_size),
        weights,
        precision=exact_mode,
    )
    fine_alpha = fine_alpha.reshape(members, levels, fine_count, block_cells)
    slab_count = levels * VARS
    pert_rows = perturbations.reshape(members, slab_count, fine_count, block_cells)
    level_ids = (
        jnp.arange(slab_count // lax.axis_size("mem") * lax.axis_size("mem"), dtype=jnp.int32)
        // VARS
    )
    alpha_rows = jnp.take(fine_alpha, level_ids, axis=1)
    increment = sent_and_summed(
        jnp.sum(pert_rows.astype(jnp.float32) * alpha_rows, axis=0), "mem", 0
    )
    slab_dev = increment.shape[0]
    obs_where = obs_cells.reshape(-1)
    flat_inc = increment.reshape(slab_dev, -1)
    observed = jnp.take(flat_inc, obs_where, axis=1)
    in_use = jnp.arange(obs_where.shape[0], dtype=jnp.int32) < obs_count.reshape(())
    weighted = jnp.where(
        in_use[None, :],
        obs_weight.reshape(slab_dev, -1) * (observed - departures.reshape(slab_dev, -1)),
        0.0,
    )
    cell_total = flat_inc.shape[1]
    all_weighted = collect(weighted, "mem", 0)
    forcing = jnp.zeros((slab_count, cell_total), jnp.float32).at[:, obs_where].add(all_weighted)
    forcing = forcing.reshape(levels, VARS, fine_count, block_cells)
    fine_gradient = jnp.sum(perturbations.astype(jnp.float32) * forcing[None], axis=2)
    contrib = jnp.einsum(
        "rfc,fkc->frk",
        fine_gradient.reshape(row_count, fine_count, block_cells),
        weights,
        precision=exact_mode,
    )
    contrib_flat = contrib.reshape(fine_count, -1)
    back_out = jnp.dot(
        selector.T, contrib_flat, precision=exact_mode, preferred_element_type=jnp.float32
    )
    returned = lax.all_to_all(
        back_out.reshape(tile_count, CAP, -1), ("tx", "ty"), split_axis=0, concat_axis=0, tiled=True
    )
    summed = jnp.einsum("dsk,dsq->kq", chooser, returned, precision=exact_mode)
    adjoint = from_blocks(summed.reshape(own_count, row_count, block_size), width_x, width_y)
    adjoint = deep_sweeps(adjoint, filter_rate, True)
    gradient = alpha + adjoint.reshape(alpha.shape)
    return (increment, weighted.reshape(departures.shape), gradient)


def solution(mesh):
    return jax.shard_map(
        on_device,
        mesh=mesh,
        in_specs=(
            P("mem", None, "tx", "ty"),
            P("tx", "ty"),
            P("tx", "ty", None),
            P("tx", "ty", None, None, None),
            P("mem", None, None, ("tx", "ty"), None),
            P("tx", "ty", None),
            P("tx", "ty"),
            P("tx", "ty", "mem", None),
            P("tx", "ty", "mem", None),
        ),
        out_specs=(
            P("mem", ("tx", "ty"), None),
            P("tx", "ty", "mem", None),
            P("mem", None, "tx", "ty"),
        ),
        check_vma=False,
    )
```

profile of v0, /device:TPU:1, one launch (start us, length us, event | category | flops | bytes accessed | tf_op | source)
XLA Modules:
  0.0 169.1 jit_solution(10911285098409685049)
XLA Ops:
  1.8 4.6 %collective-permute-start = (f32[33,4,32]{2,1,0:T(4,128)S(1)}, f32[33,4,32]{2,1,0:T(4,128)S(1)}, u32[]{:S(2)}, u32[]{:S(2)}) collective-permute-start(f32[33,4,32]{2,1,0:T(4,128)S(1)} %get-tuple-element.15), channel_id=1, source_target_pairs={{0,2},{2,4},{4,6},{6,8},{8,10},{10,12},{12,14},{1,3},{3,5},{5,7},{... | collective-permute-start | bytes 50696 | tf_op jit(solution)/shard_map/ppermute | solution.py:22
  6.4 1.9 %collective-permute-start.1 = (f32[33,4,32]{2,1,0:T(4,128)S(1)}, f32[33,4,32]{2,1,0:T(4,128)S(1)}, u32[]{:S(2)}, u32[]{:S(2)}) collective-permute-start(f32[33,4,32]{2,1,0:T(4,128)S(1)} %get-tuple-element.16), channel_id=1, source_target_pairs={{2,0},{4,2},{6,4},{8,6},{10,8},{12,10},{14,12},{3,1},{5,3},{7,5},{... | collective-permute-start | bytes 50696 | tf_op jit(solution)/shard_map/ppermute | solution.py:23
  8.3 1.3 broadcast_in_dim.57
  9.6 7.5 %all-to-all-start = ((s32[16,1,32]{2,1,0:T(1,128)}), s32[16,1,32]{2,1,0:T(1,128)S(1)}, u32[]{:S(2)}, u32[]{:S(2)}) async-start(s32[16,1,32]{2,1,0:T(1,128)} %broadcast_in_dim.57), calls=%async_computation | async-start | bytes 16384 | tf_op jit(solution)/shard_map/all_to_all | solution.py:30
  18.8 5.2 %all-to-all-done = s32[16,1,32]{2,1,0:T(1,128)S(1)} async-done(((s32[16,1,32]{2,1,0:T(1,128)}), s32[16,1,32]{2,1,0:T(1,128)S(1)}, u32[]{:S(2)}, u32[]{:S(2)}) %all-to-all-start) | async-done | bytes 2080 | tf_op jit(solution)/shard_map/all_to_all | solution.py:30
  26.6 2.2 %collective-permute-start.2 = (f32[33,24,4]{2,1,0:T(8,128)}, f32[33,24,4]{2,1,0:T(8,128)S(1)}, u32[]{:S(2)}, u32[]{:S(2)}) collective-permute-start(f32[33,24,4]{2,1,0:T(8,128)} %get-tuple-element.11), channel_id=1, source_target_pairs={{0,1},{2,3},{4,5},{6,7},{8,9},{10,11},{12,13},{14,15},{16,17},{18,... | collective-permute-start | bytes 38024 | tf_op jit(solution)/shard_map/ppermute | solution.py:22
  28.8 1.3 collective-permute-start.3
  30.3 6.8 %collective-permute-done.2 = f32[33,24,4]{2,1,0:T(8,128)S(1)} collective-permute-done((f32[33,24,4]{2,1,0:T(8,128)}, f32[33,24,4]{2,1,0:T(8,128)S(1)}, u32[]{:S(2)}, u32[]{:S(2)}) %collective-permute-start.2) | collective-permute-done | bytes 12704 | tf_op jit(solution)/shard_map/ppermute | solution.py:22
  37.1 5.0 %collective-permute-done.3 = f32[33,24,4]{2,1,0:T(8,128)S(1)} collective-permute-done((f32[33,24,4]{2,1,0:T(8,128)S(1)}, f32[33,24,4]{2,1,0:T(8,128)S(1)}, u32[]{:S(2)}, u32[]{:S(2)}) %collective-permute-start.3) | collective-permute-done | bytes 12704 | tf_op jit(solution)/shard_map/ppermute | solution.py:23
  42.1 1.3 fusion.18
  47.8 5.2 %all-to-all-start.1 = ((f32[16,2,2048]{2,1,0:T(2,128)}), f32[16,2,2048]{2,1,0:T(2,128)S(1)}, u32[]{:S(2)}, u32[]{:S(2)}) async-start(f32[16,2,2048]{2,1,0:T(2,128)} %copy.86), calls=%async_computation.1 | async-start | bytes 524288 | tf_op jit(solution)/shard_map/all_to_all | solution.py:130
  53.8 7.9 %all-to-all-done.1 = f32[16,2,2048]{2,1,0:T(2,128)S(1)} async-done(((f32[16,2,2048]{2,1,0:T(2,128)}), f32[16,2,2048]{2,1,0:T(2,128)S(1)}, u32[]{:S(2)}, u32[]{:S(2)}) %all-to-all-start.1) | async-done | bytes 262176 | tf_op jit(solution)/shard_map/all_to_all | solution.py:130
  62.8 1.5 fusion.8
  64.9 2.8 %gather_fusion.1 = f32[16,8,32,256]{3,2,1,0:T(8,128)} fusion(f32[8,4,32,256]{3,2,1,0:T(8,128)S(1)} %bitcast.92, s32[1024]{0:T(1024)S(1)} %pad_clamp_fusion.1), kind=kCustom, calls=%fused_computation.1 | custom fusion | bytes 8388672 | tf_op jit(solution)/shard_map/jit(_take)/gather | solution.py:160
  67.7 4.4 %fusion = f32[4,4,32,256]{3,2,1,0:T(8,128)} fusion(bf16[8,4,4,32,256]{4,3,2,1,0:T(8,128)(2,1)} %param.13, f32[8,4,4,32,256]{4,3,0,2,1:T(8,128)} %bitcast.93, pred[4,4]{1,0:T(4,128)(4,1)S(1)} %compare_and_fusion), kind=kLoop, calls=%fused_computation.6 | loop fusion | flops 4063232 | bytes 6815760 | tf_op jit(solution)/shard_map/reduce_sum | solution.py:162
  72.1 8.3 %all-to-all-start.2 = ((f32[16,1,32,256]{3,2,1,0:T(8,128)}), f32[16,1,32,256]{3,2,1,0:T(8,128)S(1)}, u32[]{:S(2)}, u32[]{:S(2)}) async-start(f32[16,1,32,256]{3,2,1,0:T(8,128)} %bitcast.19), calls=%async_computation.2 | async-start | bytes 1048576 | tf_op jit(solution)/shard_map/all_to_all | solution.py:54
  81.1 15.4 %all-to-all-done.2 = f32[16,1,32,256]{3,2,1,0:T(8,128)S(1)} async-done(((f32[16,1,32,256]{3,2,1,0:T(8,128)}), f32[16,1,32,256]{3,2,1,0:T(8,128)S(1)}, u32[]{:S(2)}, u32[]{:S(2)}) %all-to-all-start.2) | async-done | bytes 524320 | tf_op jit(solution)/shard_map/all_to_all | solution.py:54
  96.6 3.1 %gather_fusion.2 = f32[512]{0:T(512)S(1)} fusion(f32[8192]{0:T(1024)S(1)} %bitcast.91, s32[1024]{0:T(1024)S(1)} %pad_clamp_fusion), kind=kCustom, calls=%fused_computation.2 | custom fusion | bytes 6144 | tf_op jit(solution)/shard_map/jit(_take)/gather | solution.py:167
  100.4 4.4 %all-to-all-start.3 = ((f32[16,1,512]{2,1,0:T(1,128)}), f32[16,1,512]{2,1,0:T(1,128)S(1)}, u32[]{:S(2)}, u32[]{:S(2)}) async-start(f32[16,1,512]{2,1,0:T(1,128)} %broadcast_in_dim.66), calls=%async_computation.3 | async-start | bytes 65536 | tf_op jit(solution)/shard_map/all_to_all | solution.py:30
  104.8 7.6 %all-to-all-done.3 = f32[16,1,512]{2,1,0:T(1,128)S(1)} async-done(((f32[16,1,512]{2,1,0:T(1,128)}), f32[16,1,512]{2,1,0:T(1,128)S(1)}, u32[]{:S(2)}, u32[]{:S(2)}) %all-to-all-start.3) | async-done | bytes 32800 | tf_op jit(solution)/shard_map/all_to_all | solution.py:30
  112.5 4.4 %scatter_custom_fusion = f32[16,8192]{0,1:T(8,128)} fusion(s32[512]{0:T(512)S(1)} %bitcast.117, f32[]{:T(128)} %constant.94.clone.1, f32[16,1,512]{0,2,1:T(8,128)S(1)} %copy.100), kind=kCustom, calls=%fused_computation.14 | custom fusion | flops 8192 | bytes 786436 | tf_op jit(solution)/shard_map/scatter-add | solution.py:176
  117.0 2.8 %copy.92 = f32[16,8192]{1,0:T(8,128)S(1)} copy(f32[16,8192]{0,1:T(8,128)} %scatter_custom_fusion) | data formatting | bytes 1048576 | tf_op jit(solution)/shard_map/scatter-add | solution.py:176
  119.9 2.2 %fusion.1 = f32[8,4,32,256]{3,2,1,0:T(8,128)S(1)} fusion(bf16[8,4,4,32,256]{4,3,2,1,0:T(8,128)(2,1)} %param.13, f32[4,4,32,256]{3,2,1,0:T(8,128)S(1)} %bitcast.100), kind=kLoop, calls=%fused_computation.7 | loop fusion | flops 2883584 | bytes 3670016 | tf_op jit(solution)/shard_map/reduce_sum | solution.py:178
  122.2 2.5 %fusion.2 = f32[32,32,64]{2,1,0:T(8,128)S(1)} fusion(f32[1,1,32,64,256]{4,3,2,1,0:T(8,128)S(1)} %copy-done, f32[32,32,256]{2,1,0:T(8,128)S(1)} %bitcast.94), kind=kOutput, calls=%fused_computation.10 | convolution fusion | flops 201326592 | bytes 3407872 | tf_op jit(solution)/shard_map/rfc,fkc->frk/dot_general | solution.py:179
  125.4 15.0 %all_to_all.25 = f32[16,2,2048]{2,1,0:T(2,128)S(1)} all-to-all(f32[16,2,2048]{2,1,0:T(2,128)S(1)} %copy.94), channel_id=1, replica_groups=mesh['mem'=16,'tx'=8,'ty'=2] {'tx','ty'}, dimensions={0} | all-to-all | bytes 524288 | tf_op jit(solution)/shard_map/all_to_all | solution.py:189
  141.9 2.5 %collective-permute-start.4 = (f32[33,4,32]{2,1,0:T(4,128)S(1)}, f32[33,4,32]{2,1,0:T(4,128)S(1)}, u32[]{:S(2)}, u32[]{:S(2)}) collective-permute-start(f32[33,4,32]{2,1,0:T(4,128)S(1)} %get-tuple-element.13), channel_id=1, source_target_pairs={{0,2},{2,4},{4,6},{6,8},{8,10},{10,12},{12,14},{1,3},{3,5},{5,7},{... | collective-permute-start | bytes 50696 | tf_op jit(solution)/shard_map/ppermute | solution.py:22
  144.4 1.9 %collective-permute-start.5 = (f32[33,4,32]{2,1,0:T(4,128)S(1)}, f32[33,4,32]{2,1,0:T(4,128)S(1)}, u32[]{:S(2)}, u32[]{:S(2)}) collective-permute-start(f32[33,4,32]{2,1,0:T(4,128)S(1)} %get-tuple-element.14), channel_id=1, source_target_pairs={{2,0},{4,2},{6,4},{8,6},{10,8},{12,10},{14,12},{3,1},{5,3},{7,5},{... | collective-permute-start | bytes 50696 | tf_op jit(solution)/shard_map/ppermute | solution.py:23
  146.3 3.7 %collective-permute-done.5 = f32[33,4,32]{2,1,0:T(4,128)S(1)} collective-permute-done((f32[33,4,32]{2,1,0:T(4,128)S(1)}, f32[33,4,32]{2,1,0:T(4,128)S(1)}, u32[]{:S(2)}, u32[]{:S(2)}) %collective-permute-start.5) | collective-permute-done | bytes 16928 | tf_op jit(solution)/shard_map/ppermute | solution.py:23
  150.2 2.6 %collective-permute-start.6 = (f32[33,24,4]{2,1,0:T(8,128)S(1)}, f32[33,24,4]{2,1,0:T(8,128)S(1)}, u32[]{:S(2)}, u32[]{:S(2)}) collective-permute-start(f32[33,24,4]{2,1,0:T(8,128)S(1)} %get-tuple-element.9), channel_id=1, source_target_pairs={{0,1},{2,3},{4,5},{6,7},{8,9},{10,11},{12,13},{14,15},{16,17},{18,... | collective-permute-start | bytes 38024 | tf_op jit(solution)/shard_map/ppermute | solution.py:22
  152.9 1.3 collective-permute-start.7
  154.8 5.5 %collective-permute-done.6 = f32[33,24,4]{2,1,0:T(8,128)S(1)} collective-permute-done((f32[33,24,4]{2,1,0:T(8,128)S(1)}, f32[33,24,4]{2,1,0:T(8,128)S(1)}, u32[]{:S(2)}, u32[]{:S(2)}) %collective-permute-start.6) | collective-permute-done | bytes 12704 | tf_op jit(solution)/shard_map/ppermute | solution.py:22
  160.3 5.6 %collective-permute-done.7 = f32[33,24,4]{2,1,0:T(8,128)S(1)} collective-permute-done((f32[33,24,4]{2,1,0:T(8,128)S(1)}, f32[33,24,4]{2,1,0:T(8,128)S(1)}, u32[]{:S(2)}, u32[]{:S(2)}) %collective-permute-start.7) | collective-permute-done | bytes 12704 | tf_op jit(solution)/shard_map/ppermute | solution.py:23
  (89 shorter events, 19.6 us)
Async XLA Ops:
  0.6 62.2 %copy-start = (f32[1,1,32,64,256]{4,3,2,1,0:T(8,128)S(1)}, f32[1,1,32,64,256]{4,3,2,1,0:T(8,128)}, u32[]{:S(2)}) copy-start(f32[1,1,32,64,256]{4,3,2,1,0:T(8,128)} %param.12) | copy-start | bytes 6291460
  1.8 22.8 %collective-permute-start = (f32[33,4,32]{2,1,0:T(4,128)S(1)}, f32[33,4,32]{2,1,0:T(4,128)S(1)}, u32[]{:S(2)}, u32[]{:S(2)}) collective-permute-start(f32[33,4,32]{2,1,0:T(4,128)S(1)} %get-tuple-element.15), channel_id=1, source_target_pairs={{0,2},{2,4},{4,6},{6,8},{8,10},{10,12},{12,14},{1,3},{3,5},{5,7},{... | collective-permute-start | bytes 50696 | tf_op jit(solution)/shard_map/ppermute | solution.py:22
  6.4 18.2 %collective-permute-start.1 = (f32[33,4,32]{2,1,0:T(4,128)S(1)}, f32[33,4,32]{2,1,0:T(4,128)S(1)}, u32[]{:S(2)}, u32[]{:S(2)}) collective-permute-start(f32[33,4,32]{2,1,0:T(4,128)S(1)} %get-tuple-element.16), channel_id=1, source_target_pairs={{2,0},{4,2},{6,4},{8,6},{10,8},{12,10},{14,12},{3,1},{5,3},{7,5},{... | collective-permute-start | bytes 50696 | tf_op jit(solution)/shard_map/ppermute | solution.py:23
  9.6 14.4 %all-to-all-start = ((s32[16,1,32]{2,1,0:T(1,128)}), s32[16,1,32]{2,1,0:T(1,128)S(1)}, u32[]{:S(2)}, u32[]{:S(2)}) async-start(s32[16,1,32]{2,1,0:T(1,128)} %broadcast_in_dim.57), calls=%async_computation | async-start | bytes 16384 | tf_op jit(solution)/shard_map/all_to_all | solution.py:30
  26.6 10.5 %collective-permute-start.2 = (f32[33,24,4]{2,1,0:T(8,128)}, f32[33,24,4]{2,1,0:T(8,128)S(1)}, u32[]{:S(2)}, u32[]{:S(2)}) collective-permute-start(f32[33,24,4]{2,1,0:T(8,128)} %get-tuple-element.11), channel_id=1, source_target_pairs={{0,1},{2,3},{4,5},{6,7},{8,9},{10,11},{12,13},{14,15},{16,17},{18,... | collective-permute-start | bytes 38024 | tf_op jit(solution)/shard_map/ppermute | solution.py:22
  28.8 13.3 %collective-permute-start.3 = (f32[33,24,4]{2,1,0:T(8,128)S(1)}, f32[33,24,4]{2,1,0:T(8,128)S(1)}, u32[]{:S(2)}, u32[]{:S(2)}) collective-permute-start(f32[33,24,4]{2,1,0:T(8,128)S(1)} %get-tuple-element.12), channel_id=1, source_target_pairs={{1,0},{3,2},{5,4},{7,6},{9,8},{11,10},{13,12},{15,14},{17,16},{19,... | collective-permute-start | bytes 38024 | tf_op jit(solution)/shard_map/ppermute | solution.py:23
  30.3 14.9 %copy-start.2 = (f32[16,32]{1,0:T(8,128)S(1)}, f32[16,32]{1,0:T(8,128)}, u32[]{:S(2)}) copy-start(f32[16,32]{1,0:T(8,128)} %param.10) | copy-start | bytes 6148
  44.6 9.2 %copy-start.7 = (s32[1,1,32]{2,1,0:T(1,128)S(1)}, s32[1,1,32]{2,1,0:T(1,128)}, u32[]{:S(2)}) copy-start(s32[1,1,32]{2,1,0:T(1,128)} %param.11) | copy-start | bytes 388
  47.8 13.9 %all-to-all-start.1 = ((f32[16,2,2048]{2,1,0:T(2,128)}), f32[16,2,2048]{2,1,0:T(2,128)S(1)}, u32[]{:S(2)}, u32[]{:S(2)}) async-start(f32[16,2,2048]{2,1,0:T(2,128)} %copy.86), calls=%async_computation.1 | async-start | bytes 524288 | tf_op jit(solution)/shard_map/all_to_all | solution.py:130
  67.7 13.4 %copy-start.4 = (s32[1,1,512]{2,1,0:T(1,128)S(1)}, s32[1,1,512]{2,1,0:T(1,128)}, u32[]{:S(2)}) copy-start(s32[1,1,512]{2,1,0:T(1,128)} %param.14) | copy-start | bytes 6148
  67.7 32.0 %copy-start.5 = (f32[1,1,1,512]{3,2,1,0:T(1,128)S(1)}, f32[1,1,1,512]{3,2,1,0:T(1,128)}, u32[]{:S(2)}) copy-start(f32[1,1,1,512]{3,2,1,0:T(1,128)} %param.17) | copy-start | bytes 6148
  67.7 32.0 %copy-start.6 = (f32[1,1,1,512]{3,2,1,0:T(1,128)S(1)}, f32[1,1,1,512]{3,2,1,0:T(1,128)}, u32[]{:S(2)}) copy-start(f32[1,1,1,512]{3,2,1,0:T(1,128)} %param.16) | copy-start | bytes 6148
  72.1 24.4 %all-to-all-start.2 = ((f32[16,1,32,256]{3,2,1,0:T(8,128)}), f32[16,1,32,256]{3,2,1,0:T(8,128)S(1)}, u32[]{:S(2)}, u32[]{:S(2)}) async-start(f32[16,1,32,256]{3,2,1,0:T(8,128)} %bitcast.19), calls=%async_computation.2 | async-start | bytes 1048576 | tf_op jit(solution)/shard_map/all_to_all | solution.py:54
  96.5 23.2 %copy-start.3 = (f32[32,256]{1,0:T(8,128)}, f32[32,256]{1,0:T(8,128)S(1)}, u32[]{:S(2)}) copy-start(f32[32,256]{1,0:T(8,128)S(1)} %reduce_sum.30) | copy-start | bytes 98308
  100.4 12.0 %all-to-all-start.3 = ((f32[16,1,512]{2,1,0:T(1,128)}), f32[16,1,512]{2,1,0:T(1,128)S(1)}, u32[]{:S(2)}, u32[]{:S(2)}) async-start(f32[16,1,512]{2,1,0:T(1,128)} %broadcast_in_dim.66), calls=%async_computation.3 | async-start | bytes 65536 | tf_op jit(solution)/shard_map/all_to_all | solution.py:30
  141.9 4.4 %collective-permute-start.4 = (f32[33,4,32]{2,1,0:T(4,128)S(1)}, f32[33,4,32]{2,1,0:T(4,128)S(1)}, u32[]{:S(2)}, u32[]{:S(2)}) collective-permute-start(f32[33,4,32]{2,1,0:T(4,128)S(1)} %get-tuple-element.13), channel_id=1, source_target_pairs={{0,2},{2,4},{4,6},{6,8},{8,10},{10,12},{12,14},{1,3},{3,5},{5,7},{... | collective-permute-start | bytes 50696 | tf_op jit(solution)/shard_map/ppermute | solution.py:22
  144.4 5.6 %collective-permute-start.5 = (f32[33,4,32]{2,1,0:T(4,128)S(1)}, f32[33,4,32]{2,1,0:T(4,128)S(1)}, u32[]{:S(2)}, u32[]{:S(2)}) collective-permute-start(f32[33,4,32]{2,1,0:T(4,128)S(1)} %get-tuple-element.14), channel_id=1, source_target_pairs={{2,0},{4,2},{6,4},{8,6},{10,8},{12,10},{14,12},{3,1},{5,3},{7,5},{... | collective-permute-start | bytes 50696 | tf_op jit(solution)/shard_map/ppermute | solution.py:23
  150.2 10.0 %collective-permute-start.6 = (f32[33,24,4]{2,1,0:T(8,128)S(1)}, f32[33,24,4]{2,1,0:T(8,128)S(1)}, u32[]{:S(2)}, u32[]{:S(2)}) collective-permute-start(f32[33,24,4]{2,1,0:T(8,128)S(1)} %get-tuple-element.9), channel_id=1, source_target_pairs={{0,1},{2,3},{4,5},{6,7},{8,9},{10,11},{12,13},{14,15},{16,17},{18,... | collective-permute-start | bytes 38024 | tf_op jit(solution)/shard_map/ppermute | solution.py:22
  152.9 13.0 %collective-permute-start.7 = (f32[33,24,4]{2,1,0:T(8,128)S(1)}, f32[33,24,4]{2,1,0:T(8,128)S(1)}, u32[]{:S(2)}, u32[]{:S(2)}) collective-permute-start(f32[33,24,4]{2,1,0:T(8,128)S(1)} %get-tuple-element.10), channel_id=1, source_target_pairs={{1,0},{3,2},{5,4},{7,6},{9,8},{11,10},{13,12},{15,14},{17,16},{19,... | collective-permute-start | bytes 38024 | tf_op jit(solution)/shard_map/ppermute | solution.py:23
  167.0 1.3 copy-start.1
where the time goes:
time: 170 us; the launch traced here: 169 us
  waiting for transfers between devices  62.7 us (37%)
  starting transfers between devices  43.8 us (26%)
  other arithmetic  22.3 us (13%)
  local copies, waits for them, and re-layouts  18 us (11%)
  blocking collectives  15 us (9%)
  matrix products  5.61 us (3%)
  between operations  1.79 us (1%)
    all_to_all x1, waiting for transfers between devices, sent_and_summed(): lax.all_to_all(in_blocks(value, dim, devices), axis, 0, 0, tiled=True)  15.4 us
    all_to_all x1, blocking collectives, on_device(): lax.all_to_all(back_out.reshape(tile_count, CAP, -1), ('tx', 'ty'), split...  15 us
    ppermute x4, waiting for transfers between devices, extended(): after = lax.ppermute(leading, axis, down)  14.3 us
    all_to_all x2, waiting for transfers between devices, sent_to_all(): lax.all_to_all(jnp.broadcast_to(value[None], (devices, *value.shape)), ax...  12.8 us
    ppermute x4, waiting for transfers between devices, extended(): before = lax.ppermute(last, axis, up)  12.3 us
    ppermute x4, starting transfers between devices, extended(): before = lax.ppermute(last, axis, up)  11.9 us
    all_to_all x2, starting transfers between devices, sent_to_all(): lax.all_to_all(jnp.broadcast_to(value[None], (devices, *value.shape)), ax...  11.9 us
    all_to_all x1, starting transfers between devices, sent_and_summed(): lax.all_to_all(in_blocks(value, dim, devices), axis, 0, 0, tiled=True)  8.32 us
  transfers between devices with their start and end apart: 12, of which 9 were waited for; matrix products, arithmetic and copies ran while one was open for 3% of the time, Pallas kernels for 0%

commit v1 on v0

v1 whole, which is shorter than its diff:
```python
import jax
import jax.numpy as jnp
from jax import lax
from jax.experimental import pallas as pl
from jax.experimental.pallas import tpu as pltpu
from jax.sharding import PartitionSpec as P

MESH = pl.DeviceIdType.MESH
F32, BF16, I32 = jnp.float32, jnp.bfloat16, jnp.int32

LEV = 4
VARS = 4
CB = 8
CXC = 16
CYC = 32
SWEEPS = 4
OBS = 512
ROWS = 32
GROUPS = ROWS // 8
FINE = 32
CELLS = 256
SLABS = 16
TILES = 16
N_MEM = 16
N_TX = 8
BLOCKS = 8
LANES = 128


def lane_of(*shape):
    return lax.broadcasted_iota(I32, shape, len(shape) - 1)


def turned(value, shift):
    if isinstance(shift, int):
        shift %= LANES
        if shift == 0:
            return value
    return pltpu.roll(value, shift, axis=value.ndim - 1)


def halves(value):
    high = value.astype(BF16)
    return high, (value - high.astype(F32)).astype(BF16)


def device_halo(tx, ty):
    below, above = lax.rem(tx + N_TX - 1, N_TX), lax.rem(tx + 1, N_TX)
    return ((below, ty), (above, ty), (below, 1 - ty), (above, 1 - ty), (tx, 1 - ty))


def packed_halo(planes, ty):
    lane = lane_of(8, LANES)
    first = sum(turned(planes[j], CYC * j) for j in range(SWEEPS))
    last = sum(turned(planes[CXC - SWEEPS + j], CYC * j) for j in range(SWEEPS))
    start = (CYC - SWEEPS) * (1 - ty)
    side = 0.0
    for x in range(CXC):
        shift = lax.rem(SWEEPS * x - start + LANES, LANES)
        side = side + jnp.where(lane >> 2 == x, turned(planes[x], shift), 0.0)
    return first, last, side


def with_halo(planes, halo, tx, ty):
    lane = lane_of(8, LANES)
    own = lane < CYC
    side = (lane >> 2) == jnp.where(ty == 0, CYC // 4, LANES // 4 - 1)
    corner = jnp.where(ty == 0, CYC, 3 * CYC)
    place = jnp.where(ty == 0, CYC, LANES - SWEEPS)

    def beyond(straight, across, there):
        made = []
        for j in range(SWEEPS):
            plane = jnp.where(own, turned(straight, -CYC * j), 0.0)
            shift = lax.rem(corner - CYC * j + LANES, LANES)
            plane = plane + jnp.where(side, turned(across, shift), 0.0)
            made.append(jnp.where(there, plane, 0.0))
        return made

    low = beyond(halo[1], halo[3], tx > 0)
    high = beyond(halo[0], halo[2], tx < N_TX - 1)
    middle = []
    for x in range(CXC):
        shift = lax.rem(place - SWEEPS * x + LANES, LANES)
        middle.append(planes[x] + jnp.where(side, turned(halo[4], shift), 0.0))
    return jnp.stack(low + middle + high)


def kernel(
    block_list,
    obs_count,
    alpha,
    filter_rate,
    obs_cells,
    departures,
    obs_weight,
    weights_hbm,
    perturb_hbm,
    increment,
    weighted_out,
    gradient,
    weights,
    perturb,
    split,
    rows,
    planes,
    rates,
    select,
    halo_out,
    halo_in,
    code_out,
    code_in,
    kept,
    blocks,
    block_out,
    block_in,
    fine_a,
    fine_b,
    slab,
    slab_in,
    weighted,
    cell_hot,
    spread,
    forcing,
    contrib,
    back_out,
    back_in,
    edge_out,
    edge_in,
    load_sem,
    halo_sem,
    code_sem,
    block_sem,
    slab_sem,
    weighted_sem,
    back_sem,
    edge_sem,
):
    mem, tx, ty = lax.axis_index("mem"), lax.axis_index("tx"), lax.axis_index("ty")
    tile = tx * 2 + ty
    lane = lane_of(8, LANES)

    load_weights = pltpu.make_async_copy(weights_hbm, weights, load_sem.at[0])
    load_perturb = pltpu.make_async_copy(perturb_hbm, perturb, load_sem.at[1])
    load_weights.start()
    load_perturb.start()

    def tile_at(i):
        return lax.rem(tile + i, TILES)

    def tile_device(t):
        return {"tx": t // 2, "ty": lax.rem(t, 2)}

    def mem_at(i):
        return lax.rem(mem + i, N_MEM)

    barrier = pltpu.get_barrier_semaphore()

    def greet(i, carry):
        pl.semaphore_signal(
            barrier, inc=1, device_id=tile_device(tile_at(i)), device_id_type=MESH
        )
        pl.semaphore_signal(
            barrier, inc=1, device_id={"mem": mem_at(i)}, device_id_type=MESH
        )
        return carry

    lax.fori_loop(1, TILES, greet, 0)

    def to_tile(src, dst, sem, t, slot):
        return pltpu.make_async_remote_copy(
            src_ref=src,
            dst_ref=dst,
            send_sem=sem.at[0, t],
            recv_sem=sem.at[1, slot],
            device_id=tile_device(t),
            device_id_type=MESH,
        )

    def to_member(src, dst, sem, m, slot):
        return pltpu.make_async_remote_copy(
            src_ref=src,
            dst_ref=dst,
            send_sem=sem.at[0, m],
            recv_sem=sem.at[1, slot],
            device_id={"mem": m},
            device_id_type=MESH,
        )

    def halo_copies(out, into, sem):
        sources = (0, 1, 0, 1, 2)
        return [
            pltpu.make_async_remote_copy(
                src_ref=out.at[sources[i]],
                dst_ref=into.at[i],
                send_sem=sem.at[0, i],
                recv_sem=sem.at[1, i],
                device_id={"tx": x, "ty": y},
                device_id_type=MESH,
            )
            for i, (x, y) in enumerate(device_halo(tx, ty))
        ]

    rows[...] = jnp.zeros_like(rows)
    rows[:, 0:CYC] = alpha[...]
    rates[...] = jnp.zeros_like(rates)
    for x in range(CXC):
        planes[x] = rows[pl.ds(x, ROWS, stride=CXC), :].reshape(GROUPS, 8, LANES)
        rates[SWEEPS + x, :, 0:CYC] = jnp.broadcast_to(
            filter_rate[x : x + 1, :], (8, CYC)
        )
    both = jnp.concatenate(
        [planes[...], rates[SWEEPS : SWEEPS + CXC][:, None]], axis=1
    )
    for i, message in enumerate(packed_halo(both, ty)):
        halo_out[i] = message

    asked = lane < 0
    for f in range(FINE):
        asked = asked | (lane == block_list[0, f])
    asked = jnp.where(asked, 1.0, 0.0)
    second = jnp.zeros((8, LANES), F32)
    for j in range(1, BLOCKS):
        second = jnp.maximum(second, jnp.where((lane & 7) >= j, turned(asked, j), 0.0))
    code_out[...] = asked * (1.0 + second)

    pl.semaphore_wait(barrier, 2 * (TILES - 1))
    first_halo = halo_copies(halo_out, halo_in, halo_sem)
    for copy in first_halo:
        copy.start()

    def send_code(i, carry):
        t = tile_at(i)
        to_tile(code_out, code_in.at[tile], code_sem, t, tile).start()
        return carry

    lax.fori_loop(1, TILES, send_code, 0)
    code_in[tile] = code_out[...]

    side_half = jnp.where(lane < 64, 0.0, 1.0)
    for f in range(FINE):
        wanted = block_list[0, f]
        rank = jnp.max(jnp.where(lane == wanted, second, 0.0), axis=1, keepdims=True)
        select[f] = jnp.where(side_half == rank, wanted >> 3, -1)

    cells = obs_cells[...]
    cell_hot[...] = jnp.where(
        lax.broadcasted_iota(I32, (CELLS, OBS), 0) == (cells & (CELLS - 1)), 1.0, 0.0
    ).astype(BF16)

    def wait_code(i, carry):
        t = tile_at(i)
        to_tile(code_out, code_in.at[t], code_sem, t, t).wait_recv()
        return carry

    lax.fori_loop(1, TILES, wait_code, 0)
    lane3 = lane_of(TILES, 8, LANES)
    mine = (lane3 >> 3) == tile
    local = (lane3 & 7).astype(F32)
    codes = code_in[...]
    slot_0 = jnp.sum(jnp.where(mine & (codes == 1.0), local, 0.0), axis=2, keepdims=True)
    slot_1 = jnp.sum(jnp.where(mine & (codes == 2.0), local, 0.0), axis=2, keepdims=True)
    kept[...] = jnp.where(lane3 < 64, slot_0, slot_1)

    for copy in first_halo:
        copy.wait_recv()

    whole = with_halo(both, halo_in, tx, ty)
    field, rate = whole[:, :GROUPS], whole[:, GROUPS:]
    rates[...] = rate[:, 0]
    for sweep in range(SWEEPS):
        center = field[1:-1]
        beside = field[2:] + field[:-2] + turned(center, 1) + turned(center, -1)
        field = center + rate[1 + sweep : 23 - sweep] * (beside - 4.0 * center)

    field = jnp.where(lane < CYC, field, 0.0)
    field = (field + turned(field, 64)).reshape(2, CB, GROUPS, 8, LANES)
    for ky in range(CYC // CB):
        block = 0.0
        for x in range(CB):
            block = block + jnp.where(
                ((lane & 63) >> 3) == x, turned(field[:, x], CB * (x - ky)), 0.0
            )
        for kx in range(2):
            blocks[kx * (CYC // CB) + ky] = block[kx]

    def chosen(t):
        number = kept[t]
        block = jnp.zeros((GROUPS, 8, LANES), F32)
        for k in range(BLOCKS):
            block = jnp.where(number == float(k), blocks[k], block)
        return block

    def send_blocks(i, carry):
        t = tile_at(i)
        block_out[t] = chosen(t)
        to_tile(block_out.at[t], block_in.at[tile], block_sem, t, tile).start()
        return carry

    lax.fori_loop(1, TILES, send_blocks, 0)
    block_in[tile] = chosen(tile)

    load_weights.wait()

    def split_weights(f, carry):
        high, low = halves(weights[f])
        split[f, 0:64] = high
        split[f, 64:128] = low
        return carry

    lax.fori_loop(0, FINE, split_weights, 0)
    load_perturb.wait()

    def wait_blocks(i, carry):
        t = tile_at(i)
        to_tile(block_out.at[t], block_in.at[t], block_sem, t, t).wait_recv()
        return carry

    lax.fori_loop(1, TILES, wait_blocks, 0)

    for f in range(FINE):
        value = block_in[block_list[0, f] >> 3]
        value = jnp.where(select[f] >= 0, value, turned(value, 64))
        high, low = halves(value.reshape(ROWS, LANES))
        product = jnp.dot(
            jnp.concatenate([high, low], axis=0), split[f], preferred_element_type=F32
        )
        product = product[:ROWS] + product[ROWS:]
        fine_a[pl.ds(f, ROWS, stride=FINE), :] = product[:, :LANES]
        fine_b[pl.ds(f, ROWS, stride=FINE), :] = product[:, LANES:]

    def share(i, carry):
        level = lax.rem(mem // VARS + 1 + i, LEV)
        for half, fine in enumerate((fine_a, fine_b)):
            sums = [jnp.zeros((FINE, LANES), F32)] * VARS
            for m in range(ROWS // LEV):
                row = m * LEV + level
                value = fine[pl.ds(pl.multiple_of(row * FINE, FINE), FINE), :]
                for v in range(VARS):
                    part = perturb[row * VARS + v, :, half * LANES : (half + 1) * LANES]
                    sums[v] = sums[v] + value * part.astype(F32)
            for v in range(VARS):
                slab[level * VARS + v, :, half * LANES : (half + 1) * LANES] = sums[v]
        for v in range(VARS):
            s = level * VARS + v

            @pl.when(s != mem)
            def _():
                to_member(slab.at[s], slab_in.at[mem], slab_sem, s, mem).start()

        return carry

    lax.fori_loop(0, LEV, share, 0)

    def gather_slab(i, total):
        m = mem_at(i)
        to_member(slab.at[m], slab_in.at[m], slab_sem, m, m).wait_recv()
        return total + slab_in[m]

    total = lax.fori_loop(1, N_MEM, gather_slab, slab[mem])
    increment[...] = total

    fine_of = (cells >> 8) == lax.broadcasted_iota(I32, (FINE, OBS), 0)
    high, low = halves(total)
    at_cells = jnp.dot(
        jnp.concatenate([high, low], axis=0), cell_hot[...], preferred_element_type=F32
    )
    at_cells = at_cells[:FINE] + at_cells[FINE:]
    observed = jnp.sum(jnp.where(fine_of, at_cells, 0.0), axis=0, keepdims=True)
    in_use = lane_of(1, OBS) < obs_count[0, 0]
    residual = jnp.where(in_use, obs_weight[...] * (observed - departures[...]), 0.0)
    weighted_out[...] = residual
    weighted[mem] = residual

    def send_weighted(i, carry):
        m = mem_at(i)
        to_member(weighted.at[mem], weighted.at[mem], weighted_sem, m, mem).start()
        return carry

    lax.fori_loop(1, N_MEM, send_weighted, 0)

    def wait_weighted(i, carry):
        m = mem_at(i)
        to_member(weighted.at[m], weighted.at[m], weighted_sem, m, m).wait_recv()
        return carry

    lax.fori_loop(1, N_MEM, wait_weighted, 0)

    for s in range(SLABS):
        high, low = halves(weighted[s])
        spread[s * FINE : (s + 1) * FINE, :] = jnp.where(
            fine_of, high.astype(F32), 0.0
        ).astype(BF16)
        spread[(SLABS + s) * FINE : (SLABS + s + 1) * FINE, :] = jnp.where(
            fine_of, low.astype(F32), 0.0
        ).astype(BF16)
    forced = lax.dot_general(
        spread[...],
        cell_hot[...],
        (((1,), (1,)), ((), ())),
        preferred_element_type=F32,
    )
    forced = forced[: SLABS * FINE] + forced[SLABS * FINE :]
    forcing[...] = forced.reshape(SLABS, FINE, CELLS)

    def fine_gradient(level, carry):
        for half, fine in enumerate((fine_a, fine_b)):
            cut = slice(half * LANES, (half + 1) * LANES)
            parts = [forcing[level * VARS + v, :, cut] for v in range(VARS)]
            for m in range(ROWS // LEV):
                row = m * LEV + level
                value = sum(
                    perturb[row * VARS + v, :, cut].astype(F32) * parts[v]
                    for v in range(VARS)
                )
                fine[pl.ds(pl.multiple_of(row * FINE, FINE), FINE), :] = value
        return carry

    lax.fori_loop(0, LEV, fine_gradient, 0)

    for f in range(FINE):
        value = jnp.concatenate(
            [
                fine_a[pl.ds(f, ROWS, stride=FINE), :],
                fine_b[pl.ds(f, ROWS, stride=FINE), :],
            ],
            axis=1,
        )
        high, low = halves(value)
        product = lax.dot_general(
            jnp.concatenate([high, low], axis=0),
            split[f],
            (((1,), (1,)), ((), ())),
            preferred_element_type=F32,
        )
        product = product[:ROWS] + product[ROWS:]
        product = product + turned(product, 64)
        contrib[f] = product.reshape(GROUPS, 8, LANES)

    def returned(t):
        block = jnp.zeros((GROUPS, 8, LANES), F32)
        for f in range(FINE):
            block = block + jnp.where(select[f] == t, contrib[f], 0.0)
        return block

    def send_back(i, carry):
        t = tile_at(i)
        back_out[t] = returned(t)
        to_tile(back_out.at[t], back_in.at[tile], back_sem, t, tile).start()
        return carry

    lax.fori_loop(1, TILES, send_back, 0)
    back_in[tile] = returned(tile)

    def wait_back(i, carry):
        t = tile_at(i)
        to_tile(back_out.at[t], back_in.at[t], back_sem, t, t).wait_recv()
        return carry

    lax.fori_loop(1, TILES, wait_back, 0)

    for k in range(BLOCKS):
        block = jnp.zeros((GROUPS, 8, LANES), F32)
        for t in range(TILES):
            block = block + jnp.where(kept[t] == float(k), back_in[t], 0.0)
        blocks[k] = block + turned(block, 64)

    coarse = []
    for x in range(CXC):
        plane = 0.0
        for ky in range(CYC // CB):
            plane = plane + jnp.where(
                (lane >> 3) == ky,
                turned(blocks[x // CB * (CYC // CB) + ky], CB * (ky - x % CB)),
                0.0,
            )
        coarse.append(plane)
    for i, message in enumerate(packed_halo(coarse, ty)):
        edge_out[i] = message
    second_halo = halo_copies(edge_out, edge_in, edge_sem)
    for copy in second_halo:
        copy.start()
    for copy in second_halo:
        copy.wait_recv()
    field = with_halo(coarse, edge_in, tx, ty)
    rate = rates[...][:, None]
    for sweep in range(SWEEPS):
        scaled = rate[sweep : 24 - sweep] * field
        inner = scaled[1:-1]
        beside = scaled[2:] + scaled[:-2] + turned(inner, 1) + turned(inner, -1)
        field = field[1:-1] + beside - 4.0 * inner
    field = field + planes[...]
    for x in range(CXC):
        rows[pl.ds(x, ROWS, stride=CXC), :] = field[x].reshape(ROWS, LANES)
    gradient[...] = rows[:, 0:CYC]

    for copy in first_halo + second_halo:
        copy.wait_send()

    def wait_sent(i, carry):
        t, m = tile_at(i), mem_at(i)
        to_tile(code_out, code_in.at[tile], code_sem, t, tile).wait_send()
        to_tile(block_out.at[t], block_in.at[tile], block_sem, t, tile).wait_send()
        to_tile(back_out.at[t], back_in.at[tile], back_sem, t, tile).wait_send()
        to_member(slab.at[m], slab_in.at[mem], slab_sem, m, mem).wait_send()
        to_member(weighted.at[mem], weighted.at[mem], weighted_sem, m, mem).wait_send()
        return carry

    lax.fori_loop(1, TILES, wait_sent, 0)


def on_device(
    alpha,
    filter_rate,
    block_list,
    interp_weights,
    perturbations,
    obs_cells,
    obs_count,
    departures,
    obs_weight,
):
    in_vmem = pl.BlockSpec(memory_space=pltpu.VMEM)
    in_smem = pl.BlockSpec(memory_space=pltpu.SMEM)
    anywhere = pl.BlockSpec(memory_space=pl.ANY)
    dma = pltpu.SemaphoreType.DMA
    increment, weighted, gradient = pl.pallas_call(
        kernel,
        out_shape=(
            jax.ShapeDtypeStruct((FINE, CELLS), F32),
            jax.ShapeDtypeStruct((1, OBS), F32),
            jax.ShapeDtypeStruct((ROWS * CXC, CYC), F32),
        ),
        in_specs=[in_smem] * 2 + [in_vmem] * 5 + [anywhere] * 2,
        out_specs=(in_vmem,) * 3,
        scratch_shapes=[
            pltpu.VMEM((FINE, 64, CELLS), F32),
            pltpu.VMEM((ROWS * VARS, FINE, CELLS), BF16),
            pltpu.VMEM((FINE, 128, CELLS), BF16),
            pltpu.VMEM((ROWS * CXC, LANES), F32),
            pltpu.VMEM((CXC, GROUPS, 8, LANES), F32),
            pltpu.VMEM((CXC + 2 * SWEEPS, 8, LANES), F32),
            pltpu.VMEM((FINE, 8, LANES), I32),
            pltpu.VMEM((3, GROUPS + 1, 8, LANES), F32),
            pltpu.VMEM((5, GROUPS + 1, 8, LANES), F32),
            pltpu.VMEM((8, LANES), F32),
            pltpu.VMEM((TILES, 8, LANES), F32),
            pltpu.VMEM((TILES, 8, LANES), F32),
            pltpu.VMEM((BLOCKS, GROUPS, 8, LANES), F32),
            pltpu.VMEM((TILES, GROUPS, 8, LANES), F32),
            pltpu.VMEM((TILES, GROUPS, 8, LANES), F32),
            pltpu.VMEM((ROWS * FINE, LANES), F32),
            pltpu.VMEM((ROWS * FINE, LANES), F32),
            pltpu.VMEM((SLABS, FINE, CELLS), F32),
            pltpu.VMEM((SLABS, FINE, CELLS), F32),
            pltpu.VMEM((SLABS, 1, OBS), F32),
            pltpu.VMEM((CELLS, OBS), BF16),
            pltpu.VMEM((2 * SLABS * FINE, OBS), BF16),
            pltpu.VMEM((SLABS, FINE, CELLS), F32),
            pltpu.VMEM((FINE, GROUPS, 8, LANES), F32),
            pltpu.VMEM((TILES, GROUPS, 8, LANES), F32),
            pltpu.VMEM((TILES, GROUPS, 8, LANES), F32),
            pltpu.VMEM((3, GROUPS, 8, LANES), F32),
            pltpu.VMEM((5, GROUPS, 8, LANES), F32),
            dma((2,)),
            dma((2, 5)),
            dma((2, TILES)),
            dma((2, TILES)),
            dma((2, N_MEM)),
            dma((2, N_MEM)),
            dma((2, TILES)),
            dma((2, 5)),
        ],
        compiler_params=pltpu.CompilerParams(
            collective_id=0, has_side_effects=True, vmem_limit_bytes=40 << 20
        ),
    )(
        block_list.reshape(1, FINE),
        obs_count.reshape(1, 1),
        alpha.reshape(ROWS * CXC, CYC),
        filter_rate,
        obs_cells.reshape(1, OBS),
        departures.reshape(1, OBS),
        obs_weight.reshape(1, OBS),
        interp_weights.reshape(FINE, 64, CELLS),
        perturbations.reshape(ROWS * VARS, FINE, CELLS),
    )
    return (
        increment.reshape(1, FINE, CELLS),
        weighted.reshape(departures.shape),
        gradient.reshape(alpha.shape),
    )


def solution(mesh):
    return jax.shard_map(
        on_device,
        mesh=mesh,
        in_specs=(
            P("mem", None, "tx", "ty"),
            P("tx", "ty"),
            P("tx", "ty", None),
            P("tx", "ty", None, None, None),
            P("mem", None, None, ("tx", "ty"), None),
            P("tx", "ty", None),
            P("tx", "ty"),
            P("tx", "ty", "mem", None),
            P("tx", "ty", "mem", None),
        ),
        out_specs=(
            P("mem", ("tx", "ty"), None),
            P("tx", "ty", "mem", None),
            P("mem", None, "tx", "ty"),
        ),
        check_vma=False,
    )
```

time: 170 us -> 71.9 us (0.42)
  waiting for transfers between devices: 62.7 us -> 0 us
  Pallas kernels: 0 us -> 60.9 us
  starting transfers between devices: 43.8 us -> 0 us
  other arithmetic: 22.3 us -> 0 us
  blocking collectives: 15 us -> 0 us
  local copies, waits for them, and re-layouts: 18 us -> 9.42 us
  matrix products: 5.61 us -> 0 us
    pallas_call x0 -> x1, Pallas kernels: none -> 60.9 us  [on_device(): pl.pallas_call(kernel, out_shape=(jax.ShapeDtypeStruct((FINE, CELLS), F32...]
    all_to_all x4 -> x0, waiting for transfers between devices: 36.1 us -> none  [the longest x1 15.4 us: sent_and_summed(): lax.all_to_all(in_blocks(value, dim, devices), axis, 0, 0, tiled=True)]
    ppermute x8 -> x0, waiting for transfers between devices: 26.6 us -> none  [the longest x4 14.3 us: extended(): after = lax.ppermute(leading, axis, down)]
    all_to_all x4 -> x0, starting transfers between devices: 25.4 us -> none  [the longest x2 11.9 us: sent_to_all(): lax.all_to_all(jnp.broadcast_to(value[None], (devices, *value.shape)), ax...]
    ppermute x8 -> x0, starting transfers between devices: 18.4 us -> none  [the longest x4 11.9 us: extended(): before = lax.ppermute(last, axis, up)]
    all_to_all x1 -> x0, blocking collectives: 15 us -> none  [on_device(): lax.all_to_all(back_out.reshape(tile_count, CAP, -1), ('tx', 'ty'), split...]
    unnamed x18 -> x19, local copies, waits for them, and re-layouts: 0.22 us -> 9.42 us
    reduce_sum x3 -> x0, other arithmetic: 6.69 us -> none  [the longest x1 4.42 us: on_device(): jnp.sum(pert_rows.astype(jnp.float32) * alpha_rows, axis=0)]
  transfers between devices with their start and end apart: 12 -> 0, of which waited for: 9 -> 0; matrix products, arithmetic and copies ran while one was open for 3% -> 0% of each run, Pallas kernels for 0% -> 0%
where the time goes in v1:
time: 71.9 us; the launch traced here: 71.6 us
  Pallas kernels  60.9 us (85%)
  local copies, waits for them, and re-layouts  9.42 us (13%)
  between operations  1.3 us (2%)
    pallas_call x1, Pallas kernels, on_device(): pl.pallas_call(kernel, out_shape=(jax.ShapeDtypeStruct((FINE, CELLS), F32...  60.9 us
    unnamed x19, local copies, waits for them, and re-layouts  9.42 us

profile of v1, /device:TPU:1, one launch (start us, length us, event | category | flops | bytes accessed | tf_op | source)
XLA Modules:
  0.0 71.6 jit_solution(3462738513371878864)
XLA Ops:
  1.3 0.0 copy-start
  1.3 1.6 %copy-done = f32[1,1,32,64,256]{4,3,2,1,0:T(8,128)S(1)} copy-done((f32[1,1,32,64,256]{4,3,2,1,0:T(8,128)S(1)}, f32[1,1,32,64,256]{4,3,2,1,0:T(8,128)}, u32[]{:S(2)}) %copy-start) | copy-done | bytes 2097176
  2.9 0.0 copy-start.1
  2.9 1.6 %copy-done.1 = bf16[8,4,4,32,256]{4,3,2,1,0:T(8,128)(2,1)S(1)} copy-done((bf16[8,4,4,32,256]{4,3,2,1,0:T(8,128)(2,1)S(1)}, bf16[8,4,4,32,256]{4,3,2,1,0:T(8,128)(2,1)}, u32[]{:S(2)}) %copy-start.1) | copy-done | bytes 2097176
  4.5 0.0 copy-start.2
  4.5 0.9 %copy-done.2 = f32[8,4,16,32]{3,2,1,0:T(8,128)S(1)} copy-done((f32[8,4,16,32]{3,2,1,0:T(8,128)S(1)}, f32[8,4,16,32]{3,2,1,0:T(8,128)}, u32[]{:S(2)}) %copy-start.2) | copy-done | bytes 65560
  5.4 0.0 copy-start.3
  5.4 0.7 copy-done.3
  6.1 0.0 copy-start.4
  6.1 0.7 copy-done.4
  6.8 0.0 copy-start.5
  6.8 0.7 copy-done.5
  7.5 0.0 copy-start.6
  7.5 0.7 copy-done.6
  8.2 0.0 copy-start.7
  8.2 0.7 copy-done.7
  8.8 60.9 %shard_map.112 = (f32[32,256]{1,0:T(8,128)S(1)}, f32[1,512]{1,0:T(1,128)S(1)}, f32[512,32]{1,0:T(8,128)S(1)}) custom-call(s32[1,32]{1,0:T(1,128)S(1)} %bitcast.19, s32[1,1]{1,0:T(1,128)S(6)} %copy.15.obs_count, f32[512,32]{1,0:T(8,128)S(1)} %bitcast.13, f32[16,32]{1,0:T(8,128)S(1)} %copy-done.3, s32[1,512]{1,0:T(1,128)S(1)} %bitcast.15, ...), custom_call_target="tpu_custom_call" | custom-call | tf_op jit(solution)/shard_map/pallas_call | solution.py:527
  69.7 0.6 copy.16
  70.3 0.6 copy.17
  70.9 0.7 copy.18
Async XLA Ops:
  1.3 1.6 %copy-start = (f32[1,1,32,64,256]{4,3,2,1,0:T(8,128)S(1)}, f32[1,1,32,64,256]{4,3,2,1,0:T(8,128)}, u32[]{:S(2)}) copy-start(f32[1,1,32,64,256]{4,3,2,1,0:T(8,128)} %param.12) | copy-start | bytes 6291460
  2.9 1.6 %copy-start.1 = (bf16[8,4,4,32,256]{4,3,2,1,0:T(8,128)(2,1)S(1)}, bf16[8,4,4,32,256]{4,3,2,1,0:T(8,128)(2,1)}, u32[]{:S(2)}) copy-start(bf16[8,4,4,32,256]{4,3,2,1,0:T(8,128)(2,1)} %param.13) | copy-start | bytes 6291460
  4.5 0.9 %copy-start.2 = (f32[8,4,16,32]{3,2,1,0:T(8,128)S(1)}, f32[8,4,16,32]{3,2,1,0:T(8,128)}, u32[]{:S(2)}) copy-start(f32[8,4,16,32]{3,2,1,0:T(8,128)} %param.9) | copy-start | bytes 196612
  5.4 0.7 copy-start.3
  6.1 0.7 copy-start.4
  6.8 0.7 copy-start.5
  7.5 0.7 copy-start.6
  8.2 0.7 copy-start.7

commit v2 on v1

--- a/solution.py
+++ b/solution.py
@@ -87,6 +87,18 @@
 
 
 def kernel(
+    block_list_hbm,
+    obs_count_hbm,
+    alpha_hbm,
+    filter_rate_hbm,
+    obs_cells_hbm,
+    departures_hbm,
+    obs_weight_hbm,
+    weights_hbm,
+    perturb_hbm,
+    increment,
+    weighted_out,
+    gradient,
     block_list,
     obs_count,
     alpha,
@@ -94,11 +106,6 @@
     obs_cells,
     departures,
     obs_weight,
-    weights_hbm,
-    perturb_hbm,
-    increment,
-    weighted_out,
-    gradient,
     weights,
     perturb,
     split,
@@ -119,7 +126,10 @@
     slab,
     slab_in,
     weighted,
-    cell_hot,
+    seen_out,
+    seen_in,
+    cell_tall,
+    cell_wide,
     spread,
     forcing,
     contrib,
@@ -133,39 +143,77 @@
     block_sem,
     slab_sem,
     weighted_sem,
+    seen_sem,
     back_sem,
     edge_sem,
+    news,
 ):
     mem, tx, ty = lax.axis_index("mem"), lax.axis_index("tx"), lax.axis_index("ty")
     tile = tx * 2 + ty
     lane = lane_of(8, LANES)
-
-    load_weights = pltpu.make_async_copy(weights_hbm, weights, load_sem.at[0])
-    load_perturb = pltpu.make_async_copy(perturb_hbm, perturb, load_sem.at[1])
-    load_weights.start()
-    load_perturb.start()
+    sent = []
+
+    loads = [
+        pltpu.make_async_copy(source, target, load_sem.at[i])
+        for i, (source, target) in enumerate(
+            (
+                (alpha_hbm, alpha),
+                (filter_rate_hbm, filter_rate),
+                (block_list_hbm, block_list),
+                (obs_count_hbm, obs_count),
+                (obs_cells_hbm, obs_cells),
+                (departures_hbm, departures),
+                (obs_weight_hbm, obs_weight),
+                (weights_hbm, weights),
+                (perturb_hbm, perturb),
+            )
+        )
+    ]
+    for load in loads:
+        load.start()
+    load_weights, load_perturb = loads[7:]
+
+    y, core = lax.div(tx, 2), lax.rem(tx, 2)
+    z, run = lax.div(mem, 2), lax.rem(mem, 2)
+
+    def tile_by(dy, dcore, dty):
+        to_core = 1 - core if dcore else core
+        return (lax.rem(y + dy, 4) * 2 + to_core) * 2 + (1 - ty if dty else ty)
+
+    def mem_by(dz, drun):
+        return lax.rem(z + dz, 8) * 2 + (1 - run if drun else run)
+
+    other_tiles = [
+        tile_by(dy, dcore, dty) for dty in (1, 0) for dy in (2, 1, 3, 0) for dcore in (1, 0)
+    ][:-1]
+    other_mems = [
+        mem_by(dz, drun) for dz in (4, 3, 5, 2, 6, 1, 7, 0) for drun in (1, 0)
+    ][:-1]
 
     def tile_at(i):
         return lax.rem(tile + i, TILES)
 
     def tile_device(t):
-        return {"tx": t // 2, "ty": lax.rem(t, 2)}
+        return {"tx": lax.div(t, 2), "ty": lax.rem(t, 2)}
 
     def mem_at(i):
         return lax.rem(mem + i, N_MEM)
 
+    beside_mems = [mem_by(1, 0), mem_by(7, 0), mem_by(0, 1)]
+    two_off_mems = [mem_by(2, 0), mem_by(6, 0), mem_by(0, 1)]
     barrier = pltpu.get_barrier_semaphore()
-
-    def greet(i, carry):
+    for t in other_tiles:
         pl.semaphore_signal(
-            barrier, inc=1, device_id=tile_device(tile_at(i)), device_id_type=MESH
-        )
-        pl.semaphore_signal(
-            barrier, inc=1, device_id={"mem": mem_at(i)}, device_id_type=MESH
-        )
-        return carry
-
-    lax.fori_loop(1, TILES, greet, 0)
+            barrier, inc=1, device_id=tile_device(t), device_id_type=MESH
+        )
+    for m in beside_mems:
+        pl.semaphore_signal(barrier, inc=1, device_id={"mem": m}, device_id_type=MESH)
+
+    def tell(step, members):
+        for m in members:
+            pl.semaphore_signal(
+                news.at[step], inc=1, device_id={"mem": m}, device_id_type=MESH
+            )
 
     def to_tile(src, dst, sem, t, slot):
         return pltpu.make_async_remote_copy(
@@ -202,8 +250,10 @@
         ]
 
     rows[...] = jnp.zeros_like(rows)
+    rates[...] = jnp.zeros_like(rates)
+    for load in loads[:7]:
+        load.wait()
     rows[:, 0:CYC] = alpha[...]
-    rates[...] = jnp.zeros_like(rates)
     for x in range(CXC):
         planes[x] = rows[pl.ds(x, ROWS, stride=CXC), :].reshape(GROUPS, 8, LANES)
         rates[SWEEPS + x, :, 0:CYC] = jnp.broadcast_to(
@@ -224,17 +274,16 @@
         second = jnp.maximum(second, jnp.where((lane & 7) >= j, turned(asked, j), 0.0))
     code_out[...] = asked * (1.0 + second)
 
-    pl.semaphore_wait(barrier, 2 * (TILES - 1))
+    pl.semaphore_wait(barrier, TILES - 1 + 3)
     first_halo = halo_copies(halo_out, halo_in, halo_sem)
+    for t in other_tiles[:6]:
+        to_tile(code_out, code_in.at[tile], code_sem, t, tile).start()
     for copy in first_halo:
         copy.start()
-
-    def send_code(i, carry):
-        t = tile_at(i)
+    for t in other_tiles[6:]:
         to_tile(code_out, code_in.at[tile], code_sem, t, tile).start()
-        return carry
-
-    lax.fori_loop(1, TILES, send_code, 0)
+    tell(0, beside_mems)
+    sent.append(lambda i: to_tile(code_out, code_in.at[tile], code_sem, tile_at(i), tile))
     code_in[tile] = code_out[...]
 
     side_half = jnp.where(lane < 64, 0.0, 1.0)
@@ -244,9 +293,12 @@
         select[f] = jnp.where(side_half == rank, wanted >> 3, -1)
 
     cells = obs_cells[...]
-    cell_hot[...] = jnp.where(
+    cell_hot = jnp.where(
         lax.broadcasted_iota(I32, (CELLS, OBS), 0) == (cells & (CELLS - 1)), 1.0, 0.0
     ).astype(BF16)
+    for i in range(2):
+        cell_tall[i * CELLS : (i + 1) * CELLS, :] = cell_hot
+        cell_wide[:, i * OBS : (i + 1) * OBS] = cell_hot
 
     def wait_code(i, carry):
         t = tile_at(i)
@@ -264,6 +316,8 @@
 
     for copy in first_halo:
         copy.wait_recv()
+    pl.semaphore_wait(news.at[0], 3)
+    tell(1, two_off_mems)
 
     whole = with_halo(both, halo_in, tx, ty)
     field, rate = whole[:, :GROUPS], whole[:, GROUPS:]
@@ -291,13 +345,14 @@
             block = jnp.where(number == float(k), blocks[k], block)
         return block
 
-    def send_blocks(i, carry):
-        t = tile_at(i)
+    for t in other_tiles:
         block_out[t] = chosen(t)
         to_tile(block_out.at[t], block_in.at[tile], block_sem, t, tile).start()
-        return carry
-
-    lax.fori_loop(1, TILES, send_blocks, 0)
+    sent.append(
+        lambda i: to_tile(
+            block_out.at[tile_at(i)], block_in.at[tile], block_sem, tile_at(i), tile
+        )
+    )
     block_in[tile] = chosen(tile)
 
     load_weights.wait()
@@ -310,6 +365,8 @@
 
     lax.fori_loop(0, FINE, split_weights, 0)
     load_perturb.wait()
+    pl.semaphore_wait(news.at[1], 3)
+    tell(2, [mem_by(0, 1)])
 
     def wait_blocks(i, carry):
         t = tile_at(i)
@@ -330,7 +387,7 @@
         fine_b[pl.ds(f, ROWS, stride=FINE), :] = product[:, LANES:]
 
     def share(i, carry):
-        level = lax.rem(mem // VARS + 1 + i, LEV)
+        level = i
         for half, fine in enumerate((fine_a, fine_b)):
             sums = [jnp.zeros((FINE, LANES), F32)] * VARS
             for m in range(ROWS // LEV):
@@ -341,43 +398,55 @@
                     sums[v] = sums[v] + value * part.astype(F32)
             for v in range(VARS):
                 slab[level * VARS + v, :, half * LANES : (half + 1) * LANES] = sums[v]
-        for v in range(VARS):
-            s = level * VARS + v
-
-            @pl.when(s != mem)
-            def _():
-                to_member(slab.at[s], slab_in.at[mem], slab_sem, s, mem).start()
-
         return carry
 
     lax.fori_loop(0, LEV, share, 0)
 
-    def gather_slab(i, total):
+    fine_of = (cells >> 8) == lax.broadcasted_iota(I32, (FINE, OBS), 0)
+    high, low = halves(slab[...].reshape(SLABS * FINE, CELLS))
+    at_cells = jnp.dot(
+        jnp.concatenate([high, low], axis=1), cell_tall[...], preferred_element_type=F32
+    )
+    for s in range(SLABS):
+        here = at_cells[s * FINE : (s + 1) * FINE]
+        seen_out[s] = jnp.sum(jnp.where(fine_of, here, 0.0), axis=0, keepdims=True)
+    pl.semaphore_wait(news.at[2], 1)
+    for m in other_mems:
+        to_member(seen_out.at[m], seen_in.at[mem], seen_sem, m, mem).start()
+    sent.append(
+        lambda i: to_member(
+            seen_out.at[mem_at(i)], seen_in.at[mem], seen_sem, mem_at(i), mem
+        )
+    )
+    seen_in[mem] = seen_out[mem]
+
+    def wait_seen(i, carry):
         m = mem_at(i)
-        to_member(slab.at[m], slab_in.at[m], slab_sem, m, m).wait_recv()
-        return total + slab_in[m]
-
-    total = lax.fori_loop(1, N_MEM, gather_slab, slab[mem])
-    increment[...] = total
-
-    fine_of = (cells >> 8) == lax.broadcasted_iota(I32, (FINE, OBS), 0)
-    high, low = halves(total)
-    at_cells = jnp.dot(
-        jnp.concatenate([high, low], axis=0), cell_hot[...], preferred_element_type=F32
-    )
-    at_cells = at_cells[:FINE] + at_cells[FINE:]
-    observed = jnp.sum(jnp.where(fine_of, at_cells, 0.0), axis=0, keepdims=True)
+        to_member(seen_out.at[m], seen_in.at[m], seen_sem, m, m).wait_recv()
+        return carry
+
+    lax.fori_loop(1, N_MEM, wait_seen, 0)
+
+    observed = jnp.sum(seen_in[...], axis=0)
     in_use = lane_of(1, OBS) < obs_count[0, 0]
     residual = jnp.where(in_use, obs_weight[...] * (observed - departures[...]), 0.0)
     weighted_out[...] = residual
     weighted[mem] = residual
-
-    def send_weighted(i, carry):
-        m = mem_at(i)
+    for m in other_mems:
         to_member(weighted.at[mem], weighted.at[mem], weighted_sem, m, mem).start()
-        return carry
-
-    lax.fori_loop(1, N_MEM, send_weighted, 0)
+    sent.append(
+        lambda i: to_member(
+            weighted.at[mem], weighted.at[mem], weighted_sem, mem_at(i), mem
+        )
+    )
+
+    for m in other_mems:
+        to_member(slab.at[m], slab_in.at[mem], slab_sem, m, mem).start()
+    sent.append(
+        lambda i: to_member(
+            slab.at[mem_at(i)], slab_in.at[mem], slab_sem, mem_at(i), mem
+        )
+    )
 
     def wait_weighted(i, carry):
         m = mem_at(i)
@@ -388,19 +457,16 @@
 
     for s in range(SLABS):
         high, low = halves(weighted[s])
-        spread[s * FINE : (s + 1) * FINE, :] = jnp.where(
-            fine_of, high.astype(F32), 0.0
-        ).astype(BF16)
-        spread[(SLABS + s) * FINE : (SLABS + s + 1) * FINE, :] = jnp.where(
-            fine_of, low.astype(F32), 0.0
-        ).astype(BF16)
+        for i, part in enumerate((high, low)):
+            spread[s * FINE : (s + 1) * FINE, i * OBS : (i + 1) * OBS] = jnp.where(
+                fine_of, part.astype(F32), 0.0
+            ).astype(BF16)
     forced = lax.dot_general(
         spread[...],
-        cell_hot[...],
+        cell_wide[...],
         (((1,), (1,)), ((), ())),
         preferred_element_type=F32,
     )
-    forced = forced[: SLABS * FINE] + forced[SLABS * FINE :]
     forcing[...] = forced.reshape(SLABS, FINE, CELLS)
 
     def fine_gradient(level, carry):
@@ -443,13 +509,14 @@
             block = block + jnp.where(select[f] == t, contrib[f], 0.0)
         return block
 
-    def send_back(i, carry):
-        t = tile_at(i)
+    for t in other_tiles:
         back_out[t] = returned(t)
         to_tile(back_out.at[t], back_in.at[tile], back_sem, t, tile).start()
-        return carry
-
-    lax.fori_loop(1, TILES, send_back, 0)
+    sent.append(
+        lambda i: to_tile(
+            back_out.at[tile_at(i)], back_in.at[tile], back_sem, tile_at(i), tile
+        )
+    )
     back_in[tile] = returned(tile)
 
     def wait_back(i, carry):
@@ -494,16 +561,19 @@
         rows[pl.ds(x, ROWS, stride=CXC), :] = field[x].reshape(ROWS, LANES)
     gradient[...] = rows[:, 0:CYC]
 
+    def gather_slab(i, total):
+        m = mem_at(i)
+        to_member(slab.at[m], slab_in.at[m], slab_sem, m, m).wait_recv()
+        return total + slab_in[m]
+
+    increment[...] = lax.fori_loop(1, N_MEM, gather_slab, slab[mem])
+
     for copy in first_halo + second_halo:
         copy.wait_send()
 
     def wait_sent(i, carry):
-        t, m = tile_at(i), mem_at(i)
-        to_tile(code_out, code_in.at[tile], code_sem, t, tile).wait_send()
-        to_tile(block_out.at[t], block_in.at[tile], block_sem, t, tile).wait_send()
-        to_tile(back_out.at[t], back_in.at[tile], back_sem, t, tile).wait_send()
-        to_member(slab.at[m], slab_in.at[mem], slab_sem, m, mem).wait_send()
-        to_member(weighted.at[mem], weighted.at[mem], weighted_sem, m, mem).wait_send()
+        for of_peer in sent:
+            of_peer(i).wait_send()
         return carry
 
     lax.fori_loop(1, TILES, wait_sent, 0)
@@ -521,8 +591,7 @@
     obs_weight,
 ):
     in_vmem = pl.BlockSpec(memory_space=pltpu.VMEM)
-    in_smem = pl.BlockSpec(memory_space=pltpu.SMEM)
-    anywhere = pl.BlockSpec(memory_space=pl.ANY)
+    in_hbm = pl.BlockSpec(memory_space=pltpu.HBM)
     dma = pltpu.SemaphoreType.DMA
     increment, weighted, gradient = pl.pallas_call(
         kernel,
@@ -531,9 +600,16 @@
             jax.ShapeDtypeStruct((1, OBS), F32),
             jax.ShapeDtypeStruct((ROWS * CXC, CYC), F32),
         ),
-        in_specs=[in_smem] * 2 + [in_vmem] * 5 + [anywhere] * 2,
+        in_specs=[in_hbm] * 9,
         out_specs=(in_vmem,) * 3,
         scratch_shapes=[
+            pltpu.SMEM((1, FINE), I32),
+            pltpu.SMEM((1, 1), I32),
+            pltpu.VMEM((ROWS * CXC, CYC), F32),
+            pltpu.VMEM((CXC, CYC), F32),
+            pltpu.VMEM((1, OBS), I32),
+            pltpu.VMEM((1, OBS), F32),
+            pltpu.VMEM((1, OBS), F32),
             pltpu.VMEM((FINE, 64, CELLS), F32),
             pltpu.VMEM((ROWS * VARS, FINE, CELLS), BF16),
             pltpu.VMEM((FINE, 128, CELLS), BF16),
@@ -554,25 +630,30 @@
             pltpu.VMEM((SLABS, FINE, CELLS), F32),
             pltpu.VMEM((SLABS, FINE, CELLS), F32),
             pltpu.VMEM((SLABS, 1, OBS), F32),
-            pltpu.VMEM((CELLS, OBS), BF16),
-            pltpu.VMEM((2 * SLABS * FINE, OBS), BF16),
+            pltpu.VMEM((SLABS, 1, OBS), F32),
+            pltpu.VMEM((N_MEM, 1, OBS), F32),
+            pltpu.VMEM((2 * CELLS, OBS), BF16),
+            pltpu.VMEM((CELLS, 2 * OBS), BF16),
+            pltpu.VMEM((SLABS * FINE, 2 * OBS), BF16),
             pltpu.VMEM((SLABS, FINE, CELLS), F32),
             pltpu.VMEM((FINE, GROUPS, 8, LANES), F32),
             pltpu.VMEM((TILES, GROUPS, 8, LANES), F32),
             pltpu.VMEM((TILES, GROUPS, 8, LANES), F32),
             pltpu.VMEM((3, GROUPS, 8, LANES), F32),
             pltpu.VMEM((5, GROUPS, 8, LANES), F32),
-            dma((2,)),
+            dma((9,)),
             dma((2, 5)),
             dma((2, TILES)),
             dma((2, TILES)),
             dma((2, N_MEM)),
             dma((2, N_MEM)),
+            dma((2, N_MEM)),
             dma((2, TILES)),
             dma((2, 5)),
+            pltpu.SemaphoreType.REGULAR((3,)),
         ],
         compiler_params=pltpu.CompilerParams(
-            collective_id=0, has_side_effects=True, vmem_limit_bytes=40 << 20
+            collective_id=0, has_side_effects=True, vmem_limit_bytes=64 << 20
         ),
     )(
         block_list.reshape(1, FINE),

time: 71.9 us -> 59 us (0.82)
  Pallas kernels: 60.9 us -> 53.2 us
  local copies, waits for them, and re-layouts: 9.42 us -> 4.3 us
    pallas_call x1, Pallas kernels: 60.9 us -> 53.2 us  [on_device(): pl.pallas_call(kernel, out_shape=(jax.ShapeDtypeStruct((FINE, CELLS), F32...]
    unnamed x19 -> x3, local copies, waits for them, and re-layouts: 9.42 us -> 4.3 us
where the time goes in v2:
time: 59 us; the launch traced here: 58.8 us
  Pallas kernels  53.2 us (90%)
  local copies, waits for them, and re-layouts  4.3 us (7%)
  between operations  1.29 us (2%)
    pallas_call x1, Pallas kernels, on_device(): pl.pallas_call(kernel, out_shape=(jax.ShapeDtypeStruct((FINE, CELLS), F32...  53.2 us
    unnamed x3, local copies, waits for them, and re-layouts  4.3 us

profile of v2, /device:TPU:1, one launch (start us, length us, event | category | flops | bytes accessed | tf_op | source)
XLA Modules:
  0.0 58.8 jit_solution(12086782895103917149)
XLA Ops:
  1.3 53.2 %shard_map.112 = (f32[32,256]{1,0:T(8,128)}, f32[1,512]{1,0:T(1,128)}, f32[512,32]{1,0:T(8,128)}) custom-call(s32[1,32]{1,0:T(1,128)} %bitcast.19, s32[1,1]{1,0:T(1,128)S(6)} %copy.15.obs_count_hbm, f32[512,32]{1,0:T(8,128)} %bitcast.13, f32[16,32]{1,0:T(8,128)} %filter_rate_hbm.1, s32[1,512]{1,0:T(1,128)} %bitcast.15, f32[1,512]{1,0:T(1,128)} %bitcast.16, ...), custom_call_target="tpu_custom_call" | custom-call | tf_op jit(solution)/shard_map/pallas_call | solution.py:596
  54.5 1.4 %copy.16 = f32[1,32,256]{2,1,0:T(8,128)} copy(f32[1,32,256]{2,1,0:T(8,128)} %bitcast.14) | data formatting | bytes 65536
  55.9 1.3 %copy.17 = f32[1,1,1,512]{3,2,1,0:T(1,128)} copy(f32[1,1,1,512]{3,2,1,0:T(1,128)} %bitcast.18) | data formatting | bytes 4096
  57.1 1.7 %copy.18 = f32[8,4,16,32]{3,2,1,0:T(8,128)} copy(f32[8,4,16,32]{3,2,1,0:T(8,128)} %bitcast.12) | data formatting | bytes 131072

commit v3 on v2

--- a/solution.py
+++ b/solution.py
@@ -96,8 +96,10 @@
     obs_weight_hbm,
     weights_hbm,
     perturb_hbm,
+    increment_hbm,
+    weighted_hbm,
+    gradient_hbm,
     increment,
-    weighted_out,
     gradient,
     block_list,
     obs_count,
@@ -147,6 +149,7 @@
     back_sem,
     edge_sem,
     news,
+    store_sem,
 ):
     mem, tx, ty = lax.axis_index("mem"), lax.axis_index("tx"), lax.axis_index("ty")
     tile = tx * 2 + ty
@@ -172,6 +175,16 @@
     for load in loads:
         load.start()
     load_weights, load_perturb = loads[7:]
+    stores = [
+        pltpu.make_async_copy(source, target, store_sem.at[i])
+        for i, (source, target) in enumerate(
+            (
+                (increment, increment_hbm),
+                (weighted.at[lax.axis_index("mem")], weighted_hbm),
+                (gradient, gradient_hbm),
+            )
+        )
+    ]
 
     y, core = lax.div(tx, 2), lax.rem(tx, 2)
     z, run = lax.div(mem, 2), lax.rem(mem, 2)
@@ -430,7 +443,6 @@
     observed = jnp.sum(seen_in[...], axis=0)
     in_use = lane_of(1, OBS) < obs_count[0, 0]
     residual = jnp.where(in_use, obs_weight[...] * (observed - departures[...]), 0.0)
-    weighted_out[...] = residual
     weighted[mem] = residual
     for m in other_mems:
         to_member(weighted.at[mem], weighted.at[mem], weighted_sem, m, mem).start()
@@ -440,6 +452,15 @@
         )
     )
 
+    stores[1].start()
+
+    def wait_weighted(i, carry):
+        m = mem_at(i)
+        to_member(weighted.at[m], weighted.at[m], weighted_sem, m, m).wait_recv()
+        return carry
+
+    lax.fori_loop(1, N_MEM, wait_weighted, 0)
+
     for m in other_mems:
         to_member(slab.at[m], slab_in.at[mem], slab_sem, m, mem).start()
     sent.append(
@@ -447,13 +468,6 @@
             slab.at[mem_at(i)], slab_in.at[mem], slab_sem, mem_at(i), mem
         )
     )
-
-    def wait_weighted(i, carry):
-        m = mem_at(i)
-        to_member(weighted.at[m], weighted.at[m], weighted_sem, m, m).wait_recv()
-        return carry
-
-    lax.fori_loop(1, N_MEM, wait_weighted, 0)
 
     for s in range(SLABS):
         high, low = halves(weighted[s])
@@ -560,6 +574,7 @@
     for x in range(CXC):
         rows[pl.ds(x, ROWS, stride=CXC), :] = field[x].reshape(ROWS, LANES)
     gradient[...] = rows[:, 0:CYC]
+    stores[2].start()
 
     def gather_slab(i, total):
         m = mem_at(i)
@@ -567,6 +582,7 @@
         return total + slab_in[m]
 
     increment[...] = lax.fori_loop(1, N_MEM, gather_slab, slab[mem])
+    stores[0].start()
 
     for copy in first_halo + second_halo:
         copy.wait_send()
@@ -577,6 +593,33 @@
         return carry
 
     lax.fori_loop(1, TILES, wait_sent, 0)
+    for store in stores:
+        store.wait()
+
+
+def handed_on(*refs):
+    sources, targets, held, load_sem, store_sem = (
+        refs[:3],
+        refs[3:6],
+        refs[6:9],
+        refs[9],
+        refs[10],
+    )
+    loads = [
+        pltpu.make_async_copy(source, here, load_sem.at[i])
+        for i, (source, here) in enumerate(zip(sources, held))
+    ]
+    stores = [
+        pltpu.make_async_copy(here, target, store_sem.at[i])
+        for i, (here, target) in enumerate(zip(held, targets))
+    ]
+    for load in loads:
+        load.start()
+    for load, store in zip(loads, stores):
+        load.wait()
+        store.start()
+    for store in stores:
+        store.wait()
 
 
 def on_device(
@@ -590,19 +633,21 @@
     departures,
     obs_weight,
 ):
-    in_vmem = pl.BlockSpec(memory_space=pltpu.VMEM)
     in_hbm = pl.BlockSpec(memory_space=pltpu.HBM)
     dma = pltpu.SemaphoreType.DMA
-    increment, weighted, gradient = pl.pallas_call(
+    results = (
+        jax.ShapeDtypeStruct((FINE, CELLS), F32),
+        jax.ShapeDtypeStruct((1, OBS), F32),
+        jax.ShapeDtypeStruct((ROWS * CXC, CYC), F32),
+    )
+    made = pl.pallas_call(
         kernel,
-        out_shape=(
-            jax.ShapeDtypeStruct((FINE, CELLS), F32),
-            jax.ShapeDtypeStruct((1, OBS), F32),
-            jax.ShapeDtypeStruct((ROWS * CXC, CYC), F32),
-        ),
+        out_shape=results,
         in_specs=[in_hbm] * 9,
-        out_specs=(in_vmem,) * 3,
+        out_specs=(in_hbm,) * 3,
         scratch_shapes=[
+            pltpu.VMEM((FINE, CELLS), F32),
+            pltpu.VMEM((ROWS * CXC, CYC), F32),
             pltpu.SMEM((1, FINE), I32),
             pltpu.SMEM((1, 1), I32),
             pltpu.VMEM((ROWS * CXC, CYC), F32),
@@ -651,6 +696,7 @@
             dma((2, TILES)),
             dma((2, 5)),
             pltpu.SemaphoreType.REGULAR((3,)),
+            dma((3,)),
         ],
         compiler_params=pltpu.CompilerParams(
             collective_id=0, has_side_effects=True, vmem_limit_bytes=64 << 20
@@ -666,6 +712,15 @@
         interp_weights.reshape(FINE, 64, CELLS),
         perturbations.reshape(ROWS * VARS, FINE, CELLS),
     )
+    increment, weighted, gradient = pl.pallas_call(
+        handed_on,
+        out_shape=results,
+        in_specs=[in_hbm] * 3,
+        out_specs=(in_hbm,) * 3,
+        scratch_shapes=[pltpu.VMEM(r.shape, r.dtype) for r in results]
+        + [dma((3,)), dma((3,))],
+        compiler_params=pltpu.CompilerParams(vmem_limit_bytes=64 << 20),
+    )(*made)
     return (
         increment.reshape(1, FINE, CELLS),
         weighted.reshape(departures.shape),

time: 59 us -> 54 us (0.915)
  local copies, waits for them, and re-layouts: 4.3 us -> 0 us
  Pallas kernels: 53.2 us -> 52.6 us
    unnamed x3 -> x0, local copies, waits for them, and re-layouts: 4.3 us -> none
    pallas_call x1 -> x2, Pallas kernels: 53.2 us -> 52.6 us  [the longest x1 50.9 us: on_device(): pl.pallas_call(kernel, out_shape=results, in_specs=[in_hbm] * 9, out_spec...]
where the time goes in v3:
time: 54 us; the launch traced here: 53.9 us
  Pallas kernels  52.6 us (97%)
  between operations  1.29 us (2%)
    pallas_call x1, Pallas kernels, on_device(): pl.pallas_call(kernel, out_shape=results, in_specs=[in_hbm] * 9, out_spec...  50.9 us
    pallas_call x1, Pallas kernels, on_device(): pl.pallas_call(handed_on, out_shape=results, in_specs=[in_hbm] * 3, out_s...  1.73 us

profile of v3, /device:TPU:1, one launch (start us, length us, event | category | flops | bytes accessed | tf_op | source)
XLA Modules:
  0.0 53.9 jit_solution(2725739443850356081)
XLA Ops:
  1.3 50.9 %shard_map.112 = (f32[32,256]{1,0:T(8,128)}, f32[1,512]{1,0:T(1,128)}, f32[512,32]{1,0:T(8,128)}) custom-call(s32[1,32]{1,0:T(1,128)} %bitcast.16, s32[1,1]{1,0:T(1,128)S(6)} %copy.12.obs_count_hbm, f32[512,32]{1,0:T(8,128)} %bitcast.12, f32[16,32]{1,0:T(8,128)} %filter_rate_hbm.1, s32[1,512]{1,0:T(1,128)} %bitcast.13, f32[1,512]{1,0:T(1,128)} %bitcast.14, ...), custom_call_target="tpu_custom_call" | custom-call | tf_op jit(solution)/shard_map/pallas_call | solution.py:643
  52.2 1.7 %shard_map.113 = (f32[32,256]{1,0:T(8,128)}, f32[1,512]{1,0:T(1,128)}, f32[512,32]{1,0:T(8,128)}) custom-call(f32[32,256]{1,0:T(8,128)} %get-tuple-element.9.refs_0_, f32[1,512]{1,0:T(1,128)} %get-tuple-element.10.refs_1_, f32[512,32]{1,0:T(8,128)} %get-tuple-element.11.refs_2_), custom_call_target="tpu_custom_call" | custom-call | tf_op jit(solution)/shard_map/pallas_call | solution.py:715

commit v4 on v3

--- a/solution.py
+++ b/solution.py
@@ -20,6 +20,8 @@
 FINE = 32
 CELLS = 256
 SLABS = 16
+QUARTER = 4
+HALF = 8
 TILES = 16
 N_MEM = 16
 N_TX = 8
@@ -126,10 +128,14 @@
     fine_a,
     fine_b,
     slab,
+    paired,
+    paired_in,
     slab_in,
     weighted,
     seen_out,
     seen_in,
+    observations,
+    partial,
     cell_tall,
     cell_wide,
     spread,
@@ -143,9 +149,11 @@
     halo_sem,
     code_sem,
     block_sem,
+    pair_sem,
     slab_sem,
-    weighted_sem,
+    observed_sem,
     seen_sem,
+    partial_sem,
     back_sem,
     edge_sem,
     news,
@@ -248,6 +256,16 @@
             device_id_type=MESH,
         )
 
+    def to_member_quarter(src, dst, sem, m, theirs, mine):
+        return pltpu.make_async_remote_copy(
+            src_ref=src.at[theirs],
+            dst_ref=dst.at[mine],
+            send_sem=sem.at[0, theirs],
+            recv_sem=sem.at[1, mine],
+            device_id={"mem": m},
+            device_id_type=MESH,
+        )
+
     def halo_copies(out, into, sem):
         sources = (0, 1, 0, 1, 2)
         return [
@@ -381,6 +399,19 @@
     pl.semaphore_wait(news.at[1], 3)
     tell(2, [mem_by(0, 1)])
 
+    pl.semaphore_wait(news.at[2], 1)
+    observations[mem, 0:1, :] = departures[...]
+    observations[mem, 1:2, :] = obs_weight[...]
+    for m in other_mems:
+        to_member(
+            observations.at[mem], observations.at[mem], observed_sem, m, mem
+        ).start()
+    sent.append(
+        lambda i: to_member(
+            observations.at[mem], observations.at[mem], observed_sem, mem_at(i), mem
+        )
+    )
+
     def wait_blocks(i, carry):
         t = tile_at(i)
         to_tile(block_out.at[t], block_in.at[t], block_sem, t, t).wait_recv()
@@ -410,7 +441,8 @@
                     part = perturb[row * VARS + v, :, half * LANES : (half + 1) * LANES]
                     sums[v] = sums[v] + value * part.astype(F32)
             for v in range(VARS):
-                slab[level * VARS + v, :, half * LANES : (half + 1) * LANES] = sums[v]
+                place = v % 2 * HALF + level * 2 + v // 2
+                slab[place, :, half * LANES : (half + 1) * LANES] = sums[v]
         return carry
 
     lax.fori_loop(0, LEV, share, 0)
@@ -421,53 +453,78 @@
         jnp.concatenate([high, low], axis=1), cell_tall[...], preferred_element_type=F32
     )
     for s in range(SLABS):
-        here = at_cells[s * FINE : (s + 1) * FINE]
-        seen_out[s] = jnp.sum(jnp.where(fine_of, here, 0.0), axis=0, keepdims=True)
-    pl.semaphore_wait(news.at[2], 1)
+        place = s % 2 * HALF + s // 2
+        here = at_cells[place * FINE : (place + 1) * FINE]
+        seen_out[s // QUARTER, s % QUARTER : s % QUARTER + 1, :] = jnp.sum(
+            jnp.where(fine_of, here, 0.0), axis=0, keepdims=True
+        )
+
+    quarter = lax.rem(mem, 4)
+    z_twin = z + 1 - 2 * lax.rem(z, 2)
+    square = [z_twin * 2 + (1 - run), z_twin * 2 + run, z * 2 + (1 - run)]
+    in_square = [
+        to_member_quarter(seen_out, seen_in, seen_sem, m, lax.rem(m, 4), quarter)
+        for m in square
+    ]
+    for copy in in_square:
+        copy.start()
+    seen_in[quarter] = seen_out[quarter]
+    for m in square:
+        theirs = lax.rem(m, 4)
+        to_member_quarter(seen_out, seen_in, seen_sem, m, theirs, theirs).wait_recv()
+    partial[mem] = seen_in[0] + seen_in[1] + seen_in[2] + seen_in[3]
     for m in other_mems:
-        to_member(seen_out.at[m], seen_in.at[mem], seen_sem, m, mem).start()
+        to_member(partial.at[mem], partial.at[mem], partial_sem, m, mem).start()
     sent.append(
         lambda i: to_member(
-            seen_out.at[mem_at(i)], seen_in.at[mem], seen_sem, mem_at(i), mem
-        )
-    )
-    seen_in[mem] = seen_out[mem]
-
-    def wait_seen(i, carry):
+            partial.at[mem], partial.at[mem], partial_sem, mem_at(i), mem
+        )
+    )
+
+    def to_partner(i):
+        first = (1 - run) * HALF + 2 * i
+        return pltpu.make_async_remote_copy(
+            src_ref=slab.at[pl.ds(first, 2)],
+            dst_ref=paired_in.at[pl.ds(2 * i, 2)],
+            send_sem=pair_sem.at[0, i],
+            recv_sem=pair_sem.at[1, i],
+            device_id={"mem": mem_by(0, 1)},
+            device_id_type=MESH,
+        )
+
+    for i in range(HALF // 2):
+        to_partner(i).start()
+
+    def along_z(other, slot):
+        return pltpu.make_async_remote_copy(
+            src_ref=paired.at[other],
+            dst_ref=slab_in.at[slot],
+            send_sem=slab_sem.at[0, other],
+            recv_sem=slab_sem.at[1, slot],
+            device_id={"mem": other * 2 + run},
+            device_id_type=MESH,
+        )
+
+    def z_at(i):
+        return lax.rem(z + i, HALF)
+
+    def wait_partial(i, carry):
         m = mem_at(i)
-        to_member(seen_out.at[m], seen_in.at[m], seen_sem, m, m).wait_recv()
+        to_member(
+            observations.at[m], observations.at[m], observed_sem, m, m
+        ).wait_recv()
+        to_member(partial.at[m], partial.at[m], partial_sem, m, m).wait_recv()
         return carry
 
-    lax.fori_loop(1, N_MEM, wait_seen, 0)
-
-    observed = jnp.sum(seen_in[...], axis=0)
+    lax.fori_loop(1, N_MEM, wait_partial, 0)
+
     in_use = lane_of(1, OBS) < obs_count[0, 0]
-    residual = jnp.where(in_use, obs_weight[...] * (observed - departures[...]), 0.0)
-    weighted[mem] = residual
-    for m in other_mems:
-        to_member(weighted.at[mem], weighted.at[mem], weighted_sem, m, mem).start()
-    sent.append(
-        lambda i: to_member(
-            weighted.at[mem], weighted.at[mem], weighted_sem, mem_at(i), mem
-        )
-    )
-
+    for s in range(SLABS):
+        at, row = s // QUARTER, slice(s % QUARTER, s % QUARTER + 1)
+        seen = sum(partial[QUARTER * i + at, row, :] for i in range(4))
+        residual = observations[s, 1:2, :] * (seen - observations[s, 0:1, :])
+        weighted[s] = jnp.where(in_use, residual, 0.0)
     stores[1].start()
-
-    def wait_weighted(i, carry):
-        m = mem_at(i)
-        to_member(weighted.at[m], weighted.at[m], weighted_sem, m, m).wait_recv()
-        return carry
-
-    lax.fori_loop(1, N_MEM, wait_weighted, 0)
-
-    for m in other_mems:
-        to_member(slab.at[m], slab_in.at[mem], slab_sem, m, mem).start()
-    sent.append(
-        lambda i: to_member(
-            slab.at[mem_at(i)], slab_in.at[mem], slab_sem, mem_at(i), mem
-        )
-    )
 
     for s in range(SLABS):
         high, low = halves(weighted[s])
@@ -533,17 +590,27 @@
     )
     back_in[tile] = returned(tile)
 
-    def wait_back(i, carry):
+    for i in range(HALF // 2):
+        to_partner(i).wait_recv()
+    paired[...] = slab[pl.ds(run * HALF, HALF)] + paired_in[...]
+    for dz in (4, 3, 5, 2, 6, 1, 7):
+        along_z(z_at(dz), z).start()
+
+    def gather_back(t, blocks_so_far):
+        number, given = kept[t], back_in[t]
+        return tuple(
+            block + jnp.where(number == float(k), given, 0.0)
+            for k, block in enumerate(blocks_so_far)
+        )
+
+    def wait_back(i, blocks_so_far):
         t = tile_at(i)
         to_tile(back_out.at[t], back_in.at[t], back_sem, t, t).wait_recv()
-        return carry
-
-    lax.fori_loop(1, TILES, wait_back, 0)
-
-    for k in range(BLOCKS):
-        block = jnp.zeros((GROUPS, 8, LANES), F32)
-        for t in range(TILES):
-            block = block + jnp.where(kept[t] == float(k), back_in[t], 0.0)
+        return gather_back(t, blocks_so_far)
+
+    nothing = (jnp.zeros((GROUPS, 8, LANES), F32),) * BLOCKS
+    gathered = lax.fori_loop(1, TILES, wait_back, gather_back(tile, nothing))
+    for k, block in enumerate(gathered):
         blocks[k] = block + turned(block, 64)
 
     coarse = []
@@ -561,6 +628,15 @@
     second_halo = halo_copies(edge_out, edge_in, edge_sem)
     for copy in second_halo:
         copy.start()
+
+    def wait_sent(i, carry):
+        for of_peer in sent:
+            of_peer(i).wait_send()
+        return carry
+
+    lax.fori_loop(1, TILES, wait_sent, 0)
+    for copy in first_halo + in_square:
+        copy.wait_send()
     for copy in second_halo:
         copy.wait_recv()
     field = with_halo(coarse, edge_in, tx, ty)
@@ -577,22 +653,22 @@
     stores[2].start()
 
     def gather_slab(i, total):
-        m = mem_at(i)
-        to_member(slab.at[m], slab_in.at[m], slab_sem, m, m).wait_recv()
-        return total + slab_in[m]
-
-    increment[...] = lax.fori_loop(1, N_MEM, gather_slab, slab[mem])
+        other = z_at(i)
+        along_z(other, other).wait_recv()
+        return total + slab_in[other]
+
+    increment[...] = lax.fori_loop(1, HALF, gather_slab, paired[z])
     stores[0].start()
 
-    for copy in first_halo + second_halo:
+    def wait_slab_sent(i, carry):
+        along_z(z_at(i), z).wait_send()
+        return carry
+
+    lax.fori_loop(1, HALF, wait_slab_sent, 0)
+    for i in range(HALF // 2):
+        to_partner(i).wait_send()
+    for copy in second_halo:
         copy.wait_send()
-
-    def wait_sent(i, carry):
-        for of_peer in sent:
-            of_peer(i).wait_send()
-        return carry
-
-    lax.fori_loop(1, TILES, wait_sent, 0)
     for store in stores:
         store.wait()
 
@@ -673,10 +749,14 @@
             pltpu.VMEM((ROWS * FINE, LANES), F32),
             pltpu.VMEM((ROWS * FINE, LANES), F32),
             pltpu.VMEM((SLABS, FINE, CELLS), F32),
-            pltpu.VMEM((SLABS, FINE, CELLS), F32),
+            pltpu.VMEM((HALF, FINE, CELLS), F32),
+            pltpu.VMEM((HALF, FINE, CELLS), F32),
+            pltpu.VMEM((HALF, FINE, CELLS), F32),
             pltpu.VMEM((SLABS, 1, OBS), F32),
-            pltpu.VMEM((SLABS, 1, OBS), F32),
-            pltpu.VMEM((N_MEM, 1, OBS), F32),
+            pltpu.VMEM((4, QUARTER, OBS), F32),
+            pltpu.VMEM((4, QUARTER, OBS), F32),
+            pltpu.VMEM((N_MEM, 2, OBS), F32),
+            pltpu.VMEM((N_MEM, QUARTER, OBS), F32),
             pltpu.VMEM((2 * CELLS, OBS), BF16),
             pltpu.VMEM((CELLS, 2 * OBS), BF16),
             pltpu.VMEM((SLABS * FINE, 2 * OBS), BF16),
@@ -690,8 +770,10 @@
             dma((2, 5)),
             dma((2, TILES)),
             dma((2, TILES)),
+            dma((2, HALF // 2)),
+            dma((2, HALF)),
             dma((2, N_MEM)),
-            dma((2, N_MEM)),
+            dma((2, 4)),
             dma((2, N_MEM)),
             dma((2, TILES)),
             dma((2, 5)),

time: 54 us -> 52.5 us (0.972)
  Pallas kernels: 52.6 us -> 51.1 us
    pallas_call x1, Pallas kernels: 50.9 us -> 49.4 us  [on_device(): pl.pallas_call(kernel, out_shape=results, in_specs=[in_hbm] * 9, out_spec...]
where the time goes in v4:
time: 52.5 us; the launch traced here: 52.4 us
  Pallas kernels  51.1 us (97%)
  between operations  1.29 us (2%)
    pallas_call x1, Pallas kernels, on_device(): pl.pallas_call(kernel, out_shape=results, in_specs=[in_hbm] * 9, out_spec...  49.4 us
    pallas_call x1, Pallas kernels, on_device(): pl.pallas_call(handed_on, out_shape=results, in_specs=[in_hbm] * 3, out_s...  1.73 us

profile of v4, /device:TPU:1, one launch (start us, length us, event | category | flops | bytes accessed | tf_op | source)
XLA Modules:
  0.0 52.4 jit_solution(839630004420232161)
XLA Ops:
  1.3 49.4 %shard_map.112 = (f32[32,256]{1,0:T(8,128)}, f32[1,512]{1,0:T(1,128)}, f32[512,32]{1,0:T(8,128)}) custom-call(s32[1,32]{1,0:T(1,128)} %bitcast.16, s32[1,1]{1,0:T(1,128)S(6)} %copy.12.obs_count_hbm, f32[512,32]{1,0:T(8,128)} %bitcast.12, f32[16,32]{1,0:T(8,128)} %filter_rate_hbm.1, s32[1,512]{1,0:T(1,128)} %bitcast.13, f32[1,512]{1,0:T(1,128)} %bitcast.14, ...), custom_call_target="tpu_custom_call" | custom-call | tf_op jit(solution)/shard_map/pallas_call | solution.py:719
  50.7 1.7 %shard_map.113 = (f32[32,256]{1,0:T(8,128)}, f32[1,512]{1,0:T(1,128)}, f32[512,32]{1,0:T(8,128)}) custom-call(f32[32,256]{1,0:T(8,128)} %get-tuple-element.9.refs_0_, f32[1,512]{1,0:T(1,128)} %get-tuple-element.10.refs_1_, f32[512,32]{1,0:T(8,128)} %get-tuple-element.11.refs_2_), custom_call_target="tpu_custom_call" | custom-call | tf_op jit(solution)/shard_map/pallas_call | solution.py:797

commit v5 on v4

--- a/solution.py
+++ b/solution.py
@@ -112,6 +112,7 @@
     obs_weight,
     weights,
     perturb,
+    perturb_wide,
     split,
     rows,
     planes,
@@ -396,6 +397,13 @@
 
     lax.fori_loop(0, FINE, split_weights, 0)
     load_perturb.wait()
+
+    def widen(row, carry):
+        cut = pl.ds(pl.multiple_of(row * 4, 4), 4)
+        perturb_wide[cut] = perturb[cut].astype(F32)
+        return carry
+
+    lax.fori_loop(0, ROWS, widen, 0)
     pl.semaphore_wait(news.at[1], 3)
     tell(2, [mem_by(0, 1)])
 
@@ -438,8 +446,8 @@
                 row = m * LEV + level
                 value = fine[pl.ds(pl.multiple_of(row * FINE, FINE), FINE), :]
                 for v in range(VARS):
-                    part = perturb[row * VARS + v, :, half * LANES : (half + 1) * LANES]
-                    sums[v] = sums[v] + value * part.astype(F32)
+                    cut = slice(half * LANES, (half + 1) * LANES)
+                    sums[v] = sums[v] + value * perturb_wide[row * VARS + v, :, cut]
             for v in range(VARS):
                 place = v % 2 * HALF + level * 2 + v // 2
                 slab[place, :, half * LANES : (half + 1) * LANES] = sums[v]
@@ -547,7 +555,7 @@
             for m in range(ROWS // LEV):
                 row = m * LEV + level
                 value = sum(
-                    perturb[row * VARS + v, :, cut].astype(F32) * parts[v]
+                    perturb_wide[row * VARS + v, :, cut] * parts[v]
                     for v in range(VARS)
                 )
                 fine[pl.ds(pl.multiple_of(row * FINE, FINE), FINE), :] = value
@@ -733,6 +741,7 @@
             pltpu.VMEM((1, OBS), F32),
             pltpu.VMEM((FINE, 64, CELLS), F32),
             pltpu.VMEM((ROWS * VARS, FINE, CELLS), BF16),
+            pltpu.VMEM((ROWS * VARS, FINE, CELLS), F32),
             pltpu.VMEM((FINE, 128, CELLS), BF16),
             pltpu.VMEM((ROWS * CXC, LANES), F32),
             pltpu.VMEM((CXC, GROUPS, 8, LANES), F32),

time: 52.5 us -> 52.2 us (level)
  no operation moved by 1% of the time
where the time goes in v5:
time: 52.2 us; the launch traced here: 52 us
  Pallas kernels  50.8 us (97%)
  between operations  1.29 us (2%)
    pallas_call x1, Pallas kernels, on_device(): pl.pallas_call(kernel, out_shape=results, in_specs=[in_hbm] * 9, out_spec...  49 us
    pallas_call x1, Pallas kernels, on_device(): pl.pallas_call(handed_on, out_shape=results, in_specs=[in_hbm] * 3, out_s...  1.73 us

profile of v5, /device:TPU:1, one launch (start us, length us, event | category | flops | bytes accessed | tf_op | source)
XLA Modules:
  0.0 52.0 jit_solution(17631886096300096383)
XLA Ops:
  1.3 49.0 %shard_map.112 = (f32[32,256]{1,0:T(8,128)}, f32[1,512]{1,0:T(1,128)}, f32[512,32]{1,0:T(8,128)}) custom-call(s32[1,32]{1,0:T(1,128)} %bitcast.16, s32[1,1]{1,0:T(1,128)S(6)} %copy.12.obs_count_hbm, f32[512,32]{1,0:T(8,128)} %bitcast.12, f32[16,32]{1,0:T(8,128)} %filter_rate_hbm.1, s32[1,512]{1,0:T(1,128)} %bitcast.13, f32[1,512]{1,0:T(1,128)} %bitcast.14, ...), custom_call_target="tpu_custom_call" | custom-call | tf_op jit(solution)/shard_map/pallas_call | solution.py:727
  50.3 1.7 %shard_map.113 = (f32[32,256]{1,0:T(8,128)}, f32[1,512]{1,0:T(1,128)}, f32[512,32]{1,0:T(8,128)}) custom-call(f32[32,256]{1,0:T(8,128)} %get-tuple-element.9.refs_0_, f32[1,512]{1,0:T(1,128)} %get-tuple-element.10.refs_1_, f32[512,32]{1,0:T(8,128)} %get-tuple-element.11.refs_2_), custom_call_target="tpu_custom_call" | custom-call | tf_op jit(solution)/shard_map/pallas_call | solution.py:806
